TPU v7x, 32 devices: a whole 2x2x4 slice. The times are simulated.
32 devices in a mesh: lon: 8 (over z, x), lat: 4 (over y, core).
Axes of the slice: x: 2, y: 2, z: 4, core: 2. Of those that a mesh axis runs over, the one named last changes fastest.
Arguments:
- pressure: float32 [4, 960, 2048], P(None, 'lat', 'lon'), may hold values from -6 to 6
- wind_east: float32 [4, 960, 2048], P(None, 'lat', 'lon'), may hold values from -6 to 6
- wind_north: float32 [4, 960, 2048], P(None, 'lat', 'lon'), may hold values from -6 to 6
- forcing: float32 [4, 960, 2048], P(None, 'lat', 'lon'), may hold values from -6 to 6
- coef_lon: float32 [4, 960, 2048], P(None, 'lat', 'lon'), may hold values from 0.2 to 2
- coef_lat: float32 [4, 960, 2048], P(None, 'lat', 'lon'), may hold values from 0.2 to 2
- coef_vert: float32 [4, 960, 2048], P(None, 'lat', 'lon'), may hold values from 0.2 to 2
- diag_coef: float32 [4, 960, 2048], P(None, 'lat', 'lon'), may hold values from 0.5 to 2
Outputs:
- new_pressure: float32 [4, 960, 2048], P(None, 'lat', 'lon')
- residual: float32 [4, 960, 2048], P(None, 'lat', 'lon')
All inputs are finite; a program needn't handle non-finite values.
Results may differ from a plain program's by a relative error of at most 0.00002.
Values sent between devices are 32-bit elements; how exact they have to be, the bound alone decides.
A program may use at most 128 MiB of HBM per device.

v0:
```python
import math

import jax
import jax.numpy as jnp
from jax import lax
from jax.sharding import PartitionSpec as P


def with_halo(block, sides, width, periodic):
    for axis, dim in sides:
        count = lax.axis_size(axis)
        forward = [(i, i + 1) for i in range(count - 1)]
        if periodic:
            forward.append((count - 1, 0))
        backward = [(target, source) for source, target in forward]
        low = lax.ppermute(
            lax.slice_in_dim(block, block.shape[dim] - width, None, axis=dim), axis, forward
        )
        high = lax.ppermute(lax.slice_in_dim(block, 0, width, axis=dim), axis, backward)
        block = jnp.concatenate([low, block, high], axis=dim)
    return block


def from_behind(block, axis, distance):
    devices = range(lax.axis_size(axis))
    route = [((i - distance) % len(devices), i) for i in devices]
    return lax.ppermute(block, axis, route)


def face_cosines(start_row, face_count, lat_total):
    positions = (start_row + jnp.arange(face_count, dtype=jnp.int32)).astype(jnp.float32)
    return jnp.cos(positions * (math.pi / lat_total) - math.pi / 2)


def divergence(east_ext, north_ext, face_cos):
    cos_low = face_cos[:-1][None, :, None]
    cos_high = face_cos[1:][None, :, None]
    middle = north_ext[:, 1:-1, 1:-1]
    zonal = 0.5 * (east_ext[:, 1:-1, 2:] - east_ext[:, 1:-1, :-2])
    merid = 0.5 * (
        cos_high * (middle + north_ext[:, 2:, 1:-1]) - cos_low * (north_ext[:, :-2, 1:-1] + middle)
    )
    return zonal + merid


def helmholtz(field_ext, lon_ext, lat_ext, vert_coef, diag_coef, face_cos):
    centre = field_ext[:, 1:-1, 1:-1]
    lon_mid = lon_ext[:, 1:-1, 1:-1]
    west_weight = 0.5 * (lon_mid + lon_ext[:, 1:-1, :-2])
    east_weight = 0.5 * (lon_mid + lon_ext[:, 1:-1, 2:])
    metric = 0.5 * (1.0 + jnp.abs(face_cos))
    lat_mid = lat_ext[:, 1:-1, 1:-1]
    south_weight = metric[:-1][None, :, None] * (0.5 * (lat_mid + lat_ext[:, :-2, 1:-1]))
    north_weight = metric[1:][None, :, None] * (0.5 * (lat_mid + lat_ext[:, 2:, 1:-1]))
    zero_level = jnp.zeros_like(centre[:1])
    upper_weight = jnp.concatenate((vert_coef[1:], jnp.zeros_like(vert_coef[:1])), 0)
    below = jnp.concatenate((zero_level, centre[:-1]), 0)
    above = jnp.concatenate((centre[1:], zero_level), 0)
    diag_total = (
        diag_coef
        + west_weight
        + east_weight
        + south_weight
        + north_weight
        + vert_coef
        + upper_weight
    )
    coupled = (
        west_weight * field_ext[:, 1:-1, :-2]
        + east_weight * field_ext[:, 1:-1, 2:]
        + south_weight * field_ext[:, :-2, 1:-1]
        + north_weight * field_ext[:, 2:, 1:-1]
        + vert_coef * below
        + upper_weight * above
    )
    return (diag_total * centre - coupled, diag_total)


def place_poles(latitude, partner, rim_width):
    lat_index = lax.axis_index("lat")
    lat_devices = lax.axis_size("lat")
    south_rim = jnp.where(lat_index == 0, partner[0], latitude[:, :, :rim_width])
    north_rim = jnp.where(lat_index == lat_devices - 1, partner[1], latitude[:, :, -rim_width:])
    return jnp.concatenate((south_rim, latitude[:, :, rim_width:-rim_width], north_rim), 2)


def pole_edges(stacked, rim_width):
    return jnp.stack(
        (jnp.flip(stacked[:, :, :rim_width], 2), jnp.flip(stacked[:, :, -rim_width:], 2))
    )


def extend_rows(stacked, rim_width):
    latitude = with_halo(stacked, (("lat", 2),), rim_width, False)
    partner = from_behind(pole_edges(stacked, rim_width), "lon", lax.axis_size("lon") // 2)
    latitude = place_poles(latitude, partner, rim_width)
    return with_halo(latitude, (("lon", 3),), rim_width, True)


def per_device(pressure, wind_east, wind_north, forcing, coef_lon, coef_lat, coef_vert, diag_coef):
    lat_rows = pressure.shape[1]
    lat_total = lat_rows * lax.axis_size("lat")
    start_row = lax.axis_index("lat") * lat_rows
    face_cos = face_cosines(start_row, lat_rows + 1, lat_total)
    extended = extend_rows(jnp.stack((pressure, wind_east, wind_north, coef_lon, coef_lat)), 1)
    rhs_field = forcing - divergence(extended[1], extended[2], face_cos)
    applied, diag_total = helmholtz(
        extended[0], extended[3], extended[4], coef_vert, diag_coef, face_cos
    )
    new_pressure = pressure + (rhs_field - applied) / diag_total
    pressure_ext = extend_rows(new_pressure[None], 1)[0]
    applied_new, unused = helmholtz(
        pressure_ext, extended[3], extended[4], coef_vert, diag_coef, face_cos
    )
    return (new_pressure, rhs_field - applied_new)


def solution(mesh):
    in_specs = (
        P(None, "lat", "lon"),
        P(None, "lat", "lon"),
        P(None, "lat", "lon"),
        P(None, "lat", "lon"),
        P(None, "lat", "lon"),
        P(None, "lat", "lon"),
        P(None, "lat", "lon"),
        P(None, "lat", "lon"),
    )
    out_specs = (P(None, "lat", "lon"), P(None, "lat", "lon"))
    return jax.shard_map(
        per_device, mesh=mesh, in_specs=in_specs, out_specs=out_specs, check_vma=False
    )
```

profile of v0, /device:TPU:0, one launch (start us, length us, event | category | flops | bytes accessed | tf_op | source)
XLA Modules:
  0.0 106.0 jit_solution(8060007261457158701)
XLA Ops:
  0.7 2.0 %bitcast_dynamic-update-slice_fusion.4 = f32[5,4,240,256]{3,1,0,2:T(4,128)S(1)} fusion(f32[4,240,256]{2,1,0:T(8,128)} %param.8), kind=kLoop, calls=%fused_computation.55 | loop fusion | bytes 1966080
  2.7 0.7 bitcast_dynamic-update-slice_fusion.3
  4.1 0.7 bitcast_dynamic-update-slice_fusion.1
  5.5 2.2 %copy-done = f32[5,4,240,256]{3,1,0,2:T(4,128)} copy-done((f32[5,4,240,256]{3,1,0,2:T(4,128)}, f32[5,4,240,256]{3,1,0,2:T(4,128)S(1)}, u32[]{:S(2)}) %copy-start) | copy-done | bytes 4915224
  7.8 4.1 %collective-permute-start = (f32[2,5,4,1,256]{4,2,1,3,0:T(4,128)S(1)}, f32[2,5,4,1,256]{4,2,1,3,0:T(4,128)S(1)}, u32[]{:S(2)}, u32[]{:S(2)}) collective-permute-start(f32[2,5,4,1,256]{4,2,1,3,0:T(4,128)S(1)} %pad_maximum_fusion.3), channel_id=1, source_target_pairs={{16,0},{20,4},{24,8},{28,12},{0,16},{4,20},{8,24},{12,28},{17,1},{... | collective-permute-start | bytes 122888 | tf_op jit(solution)/shard_map/ppermute | solution.py:27
  11.9 1.4 %collective-permute-start.1 = (f32[5,4,1,256]{3,1,0,2:T(4,128)S(1)}, f32[5,4,1,256]{3,1,0,2:T(4,128)S(1)}, u32[]{:S(2)}, u32[]{:S(2)}) collective-permute-start(f32[5,4,1,256]{3,1,0,2:T(4,128)S(1)} %get-tuple-element.15), channel_id=1, source_target_pairs={{0,1},{1,2},{2,3},{4,5},{5,6},{6,7},{8,9},{9,10},{10,11},{12,13},{... | collective-permute-start | bytes 61448 | tf_op jit(solution)/shard_map/ppermute | solution.py:16
  13.3 1.3 %collective-permute-start.2 = (f32[5,4,1,256]{3,1,0,2:T(4,128)S(1)}, f32[5,4,1,256]{3,1,0,2:T(4,128)S(1)}, u32[]{:S(2)}, u32[]{:S(2)}) collective-permute-start(f32[5,4,1,256]{3,1,0,2:T(4,128)S(1)} %get-tuple-element.18), channel_id=1, source_target_pairs={{1,0},{2,1},{3,2},{5,4},{6,5},{7,6},{9,8},{10,9},{11,10},{13,12},{... | collective-permute-start | bytes 61448 | tf_op jit(solution)/shard_map/ppermute | solution.py:19
  14.8 3.2 %collective-permute-done.2 = f32[5,4,1,256]{3,1,0,2:T(4,128)S(1)} collective-permute-done((f32[5,4,1,256]{3,1,0,2:T(4,128)S(1)}, f32[5,4,1,256]{3,1,0,2:T(4,128)S(1)}, u32[]{:S(2)}, u32[]{:S(2)}) %collective-permute-start.2) | collective-permute-done | bytes 20512 | tf_op jit(solution)/shard_map/ppermute | solution.py:19
  18.0 3.5 %pad_maximum_fusion.1 = f32[5,4,242,256]{3,1,0,2:T(4,128)S(1)} fusion(f32[5,4,1,256]{3,1,0,2:T(4,128)S(1)} %get-tuple-element.30, f32[5,4,240,256]{3,1,0,2:T(4,128)} %copy-done, f32[5,4,1,256]{3,1,0,2:T(4,128)S(1)} %get-tuple-element.29), kind=kLoop, calls=%fused_computation.1 | loop fusion | flops 2478080 | bytes 9912320 | tf_op jit(solution)/shard_map/concatenate | solution.py:84
  21.5 3.1 %fusion.36 = (f32[5,4,242,1]{3,1,0,2:T(4,128)}, f32[5,4,242,1]{3,1,0,2:T(4,128)S(1)}) fusion(f32[5,4,242,256]{3,1,0,2:T(4,128)S(1)} %pad_maximum_fusion.1), kind=kLoop, calls=%fused_computation.81 | loop fusion | bytes 77440 | tf_op jit(solution)/shard_map/slice | solution.py:17
  24.6 2.2 %copy.36 = f32[5,4,242,1]{2,1,3,0:T(4,128)S(1)} copy(f32[5,4,242,1]{3,1,0,2:T(4,128)} %get-tuple-element.13) | data formatting | bytes 38720 | tf_op jit(solution)/shard_map/slice | solution.py:17
  26.8 1.5 %collective-permute-start.3 = (f32[5,4,242,1]{2,1,3,0:T(4,128)S(1)}, f32[5,4,242,1]{2,1,3,0:T(4,128)S(1)}, u32[]{:S(2)}, u32[]{:S(2)}) collective-permute-start(f32[5,4,242,1]{2,1,3,0:T(4,128)S(1)} %copy.36), channel_id=1, source_target_pairs={{0,4},{4,8},{8,12},{12,16},{16,20},{20,24},{24,28},{28,0},{1,5},{5... | collective-permute-start | bytes 58088 | tf_op jit(solution)/shard_map/ppermute | solution.py:16
  28.3 2.2 %copy.37 = f32[5,4,242,1]{2,1,3,0:T(4,128)} copy(f32[5,4,242,1]{3,1,0,2:T(4,128)S(1)} %get-tuple-element.14) | data formatting | bytes 38720 | tf_op jit(solution)/shard_map/slice | solution.py:19
  30.6 3.2 %collective-permute-start.4 = (f32[5,4,242,1]{2,1,3,0:T(4,128)}, f32[5,4,242,1]{2,1,3,0:T(4,128)}, u32[]{:S(2)}, u32[]{:S(2)}) collective-permute-start(f32[5,4,242,1]{2,1,3,0:T(4,128)} %copy.37), channel_id=1, source_target_pairs={{4,0},{8,4},{12,8},{16,12},{20,16},{24,20},{28,24},{0,28},{5,1},{9... | collective-permute-start | bytes 58088 | tf_op jit(solution)/shard_map/ppermute | solution.py:19
  35.0 1.7 %copy.38 = f32[5,4,242,1]{3,1,0,2:T(4,128)S(1)} copy(f32[5,4,242,1]{2,1,3,0:T(4,128)S(1)} %collective-permute-done.3) | data formatting | bytes 38720 | tf_op jit(solution)/shard_map/ppermute | solution.py:16
  36.8 2.6 %copy.39 = f32[5,4,242,1]{3,1,0,2:T(4,128)} copy(f32[5,4,242,1]{2,1,3,0:T(4,128)} %collective-permute-done.4) | data formatting | bytes 38720 | tf_op jit(solution)/shard_map/ppermute | solution.py:19
  39.4 13.0 %pad_maximum_fusion = f32[5,4,242,258]{3,1,0,2:T(4,128)S(1)} fusion(f32[5,4,242,1]{3,1,0,2:T(4,128)} %copy.39, f32[5,4,1,256]{3,1,0,2:T(4,128)S(1)} %get-tuple-element.30, f32[5,4,240,256]{3,1,0,2:T(4,128)} %copy-done, f32[5,4,1,256]{3,1,0,2:T(4,128)S(1)} %get-tuple-element.29, f32[5,4,242,1]{3,1,0,2:T(4,128)S(1)} %copy.38), kind=kLoop, calls=%fused_computation | loop fusion | flops 4994880 | bytes 9989760 | tf_op jit(solution)/shard_map/concatenate | solution.py:20
  52.4 1.3 %slice_bitcast_fusion.4 = (f32[4,242,258]{2,0,1:T(4,128)S(1)}, f32[4,242,258]{2,0,1:T(4,128)S(1)}, f32[4,242,258]{2,0,1:T(4,128)S(1)}, f32[4,242,258]{2,0,1:T(4,128)S(1)}, f32[4,242,258]{2,0,1:T(4,128)S(1)}) fusion(f32[5,4,242,258]{3,1,0,2:T(4,128)S(1)} %pad_maximum_fusion), kind=kLoop, calls=%fused_computation.6 | loop fusion | bytes 9989760 | tf_op jit(solution)/shard_map/squeeze | solution.py:106
  53.8 1.1 %fusion.39 = (f32[3,240,256]{2,0,1:T(4,128)S(1)}, f32[3,240,256]{2,0,1:T(4,128)S(1)}) fusion(f32[4,242,258]{2,0,1:T(4,128)S(1)} %get-tuple-element.11), kind=kLoop, calls=%fused_computation.84 | loop fusion | bytes 2949120 | tf_op jit(solution)/shard_map/slice | solution.py:57
  55.8 9.1 %fusion.30 = (f32[4,240,256]{2,0,1:T(4,128)S(1)}, f32[4,240,256]{2,0,1:T(4,128)S(1)}) fusion(f32[3,240,256]{2,0,1:T(4,128)S(1)} %get-tuple-element.22, f32[3,240,256]{2,0,1:T(4,128)S(1)} %get-tuple-element.21, f32[4,242,258]{2,0,1:T(4,128)S(1)} %get-tuple-element.11, f32[4,240,256]{2,1,0:T(8,128)S(1)} %copy-done.4, f32[4,240,256]{2,1,0:T(8,128)S(1)} %copy-done.3, ...), kind=kLoop, calls=%fused_computation.62 | loop fusion | flops 9584640 | bytes 23842560 | tf_op jit(solution)/shard_map/add | solution.py:110
  65.0 3.9 %collective-permute-start.6 = (f32[1,4,1,256]{3,1,2,0:T(4,128)S(1)}, f32[1,4,1,256]{3,1,2,0:T(4,128)S(1)}, u32[]{:S(2)}, u32[]{:S(2)}) collective-permute-start(f32[1,4,1,256]{3,1,2,0:T(4,128)S(1)} %get-tuple-element.25), channel_id=1, source_target_pairs={{0,1},{1,2},{2,3},{4,5},{5,6},{6,7},{8,9},{9,10},{10,11},{12,13},{... | collective-permute-start | bytes 12296 | tf_op jit(solution)/shard_map/ppermute | solution.py:16
  68.9 1.3 %collective-permute-start.7 = (f32[1,4,1,256]{3,1,2,0:T(4,128)S(1)}, f32[1,4,1,256]{3,1,2,0:T(4,128)S(1)}, u32[]{:S(2)}, u32[]{:S(2)}) collective-permute-start(f32[1,4,1,256]{3,1,2,0:T(4,128)S(1)} %get-tuple-element.28), channel_id=1, source_target_pairs={{1,0},{2,1},{3,2},{5,4},{6,5},{7,6},{9,8},{10,9},{11,10},{13,12},{... | collective-permute-start | bytes 12296 | tf_op jit(solution)/shard_map/ppermute | solution.py:19
  70.2 1.8 %collective-permute-done.7 = f32[1,4,1,256]{3,1,2,0:T(4,128)S(1)} collective-permute-done((f32[1,4,1,256]{3,1,2,0:T(4,128)S(1)}, f32[1,4,1,256]{3,1,2,0:T(4,128)S(1)}, u32[]{:S(2)}, u32[]{:S(2)}) %collective-permute-start.7) | collective-permute-done | bytes 4128 | tf_op jit(solution)/shard_map/ppermute | solution.py:19
  72.6 0.7 collective-permute-start.8
  73.3 4.1 %collective-permute-start.9 = (f32[1,4,242,1]{3,1,2,0:T(4,128)S(1)}, f32[1,4,242,1]{3,1,2,0:T(4,128)S(1)}, u32[]{:S(2)}, u32[]{:S(2)}) collective-permute-start(f32[1,4,242,1]{3,1,2,0:T(4,128)S(1)} %get-tuple-element.24), channel_id=1, source_target_pairs={{4,0},{8,4},{12,8},{16,12},{20,16},{24,20},{28,24},{0,28},{5,1},{9... | collective-permute-start | bytes 11624 | tf_op jit(solution)/shard_map/ppermute | solution.py:19
  77.3 1.1 %copy.51 = f32[4,240,256]{2,1,0:T(8,128)} copy(f32[4,240,256]{2,0,1:T(4,128)S(1)} %get-tuple-element.6) | data formatting | bytes 1966080
  78.5 15.7 %collective-permute-done.8 = f32[1,4,242,1]{3,1,2,0:T(4,128)S(1)} collective-permute-done((f32[1,4,242,1]{3,1,2,0:T(4,128)S(1)}, f32[1,4,242,1]{3,1,2,0:T(4,128)S(1)}, u32[]{:S(2)}, u32[]{:S(2)}) %collective-permute-start.8) | collective-permute-done | bytes 3904 | tf_op jit(solution)/shard_map/ppermute | solution.py:16
  94.1 2.8 %collective-permute-done.9 = f32[1,4,242,1]{3,1,2,0:T(4,128)S(1)} collective-permute-done((f32[1,4,242,1]{3,1,2,0:T(4,128)S(1)}, f32[1,4,242,1]{3,1,2,0:T(4,128)S(1)}, u32[]{:S(2)}, u32[]{:S(2)}) %collective-permute-start.9) | collective-permute-done | bytes 3904 | tf_op jit(solution)/shard_map/ppermute | solution.py:19
  96.9 1.1 %maximum_bitcast_fusion = f32[4,242,258]{2,0,1:T(4,128)S(1)} fusion(f32[1,4,242,1]{3,1,2,0:T(4,128)S(1)} %collective-permute-done.9, f32[1,4,1,256]{3,1,2,0:T(4,128)S(1)} %get-tuple-element.32, f32[1,4,240,256]{3,1,2,0:T(4,128)S(1)} %bitcast.57, f32[1,4,1,256]{3,1,2,0:T(4,128)S(1)} %get-tuple-element.31, f32[1,4,242,1]{3,1,2,0:T(4,128)S(1)} %collective-permute-done.8), kind=kLoop, calls=%fused_computation.7 | loop fusion | flops 998976 | bytes 1997952 | tf_op jit(solution)/shard_map/squeeze | solution.py:111
  98.0 1.1 %fusion.38 = (f32[3,240,256]{2,0,1:T(4,128)S(1)}, f32[3,240,256]{2,0,1:T(4,128)S(1)}) fusion(f32[4,242,258]{2,0,1:T(4,128)S(1)} %maximum_bitcast_fusion), kind=kLoop, calls=%fused_computation.83 | loop fusion | bytes 2949120 | tf_op jit(solution)/shard_map/slice | solution.py:57
  99.1 5.8 %fusion.4 = f32[4,240,256]{2,0,1:T(4,128)S(1)} fusion(f32[4,240,256]{2,0,1:T(4,128)S(1)} %get-tuple-element.7, f32[4,242,258]{2,0,1:T(4,128)S(1)} %maximum_bitcast_fusion, f32[4,240,256]{2,1,0:T(8,128)S(1)} %copy-done.4, f32[3,240,256]{2,0,1:T(4,128)S(1)} %get-tuple-element.20, f32[3,240,256]{2,0,1:T(4,128)S(1)} %get-tuple-element.19, ...), kind=kLoop, calls=%fused_computation.14 | loop fusion | flops 6881280 | bytes 16959360 | tf_op jit(solution)/shard_map/sub | solution.py:115
  104.9 1.1 %copy.52 = f32[4,240,256]{2,1,0:T(8,128)} copy(f32[4,240,256]{2,0,1:T(4,128)S(1)} %fusion.4) | data formatting | bytes 1966080
  (45 shorter events, 4.4 us)
Async XLA Ops:
  0.6 2.0 %copy-start.5 = (f32[4,240,256]{2,1,0:T(8,128)S(1)}, f32[4,240,256]{2,1,0:T(8,128)}, u32[]{:S(2)}) copy-start(f32[4,240,256]{2,1,0:T(8,128)} %param.9) | copy-start | bytes 2949124
  0.6 2.7 %copy-start.6 = (f32[4,240,256]{2,1,0:T(8,128)S(1)}, f32[4,240,256]{2,1,0:T(8,128)}, u32[]{:S(2)}) copy-start(f32[4,240,256]{2,1,0:T(8,128)} %param.10) | copy-start | bytes 2949124
  0.7 3.4 %copy-start.7 = (f32[4,240,256]{2,1,0:T(8,128)S(1)}, f32[4,240,256]{2,1,0:T(8,128)}, u32[]{:S(2)}) copy-start(f32[4,240,256]{2,1,0:T(8,128)} %param.12) | copy-start | bytes 2949124
  2.7 2.1 %copy-start.8 = (f32[4,240,256]{2,1,0:T(8,128)S(1)}, f32[4,240,256]{2,1,0:T(8,128)}, u32[]{:S(2)}) copy-start(f32[4,240,256]{2,1,0:T(8,128)} %param.13) | copy-start | bytes 2949124
  5.5 2.2 %copy-start = (f32[5,4,240,256]{3,1,0,2:T(4,128)}, f32[5,4,240,256]{3,1,0,2:T(4,128)S(1)}, u32[]{:S(2)}) copy-start(f32[5,4,240,256]{3,1,0,2:T(4,128)S(1)} %bitcast_dynamic-update-slice_fusion) | copy-start | bytes 14745604
  7.8 10.2 %collective-permute-start = (f32[2,5,4,1,256]{4,2,1,3,0:T(4,128)S(1)}, f32[2,5,4,1,256]{4,2,1,3,0:T(4,128)S(1)}, u32[]{:S(2)}, u32[]{:S(2)}) collective-permute-start(f32[2,5,4,1,256]{4,2,1,3,0:T(4,128)S(1)} %pad_maximum_fusion.3), channel_id=1, source_target_pairs={{16,0},{20,4},{24,8},{28,12},{0,16},{4,20},{8,24},{12,28},{17,1},{... | collective-permute-start | bytes 122888 | tf_op jit(solution)/shard_map/ppermute | solution.py:27
  11.9 2.9 %collective-permute-start.1 = (f32[5,4,1,256]{3,1,0,2:T(4,128)S(1)}, f32[5,4,1,256]{3,1,0,2:T(4,128)S(1)}, u32[]{:S(2)}, u32[]{:S(2)}) collective-permute-start(f32[5,4,1,256]{3,1,0,2:T(4,128)S(1)} %get-tuple-element.15), channel_id=1, source_target_pairs={{0,1},{1,2},{2,3},{4,5},{5,6},{6,7},{8,9},{9,10},{10,11},{12,13},{... | collective-permute-start | bytes 61448 | tf_op jit(solution)/shard_map/ppermute | solution.py:16
  13.3 4.7 %collective-permute-start.2 = (f32[5,4,1,256]{3,1,0,2:T(4,128)S(1)}, f32[5,4,1,256]{3,1,0,2:T(4,128)S(1)}, u32[]{:S(2)}, u32[]{:S(2)}) collective-permute-start(f32[5,4,1,256]{3,1,0,2:T(4,128)S(1)} %get-tuple-element.18), channel_id=1, source_target_pairs={{1,0},{2,1},{3,2},{5,4},{6,5},{7,6},{9,8},{10,9},{11,10},{13,12},{... | collective-permute-start | bytes 61448 | tf_op jit(solution)/shard_map/ppermute | solution.py:19
  24.6 9.8 %copy-start.1 = (f32[4,240,256]{2,1,0:T(8,128)S(1)}, f32[4,240,256]{2,1,0:T(8,128)}, u32[]{:S(2)}) copy-start(f32[4,240,256]{2,1,0:T(8,128)} %param.14) | copy-start | bytes 2949124
  26.8 8.2 %collective-permute-start.3 = (f32[5,4,242,1]{2,1,3,0:T(4,128)S(1)}, f32[5,4,242,1]{2,1,3,0:T(4,128)S(1)}, u32[]{:S(2)}, u32[]{:S(2)}) collective-permute-start(f32[5,4,242,1]{2,1,3,0:T(4,128)S(1)} %copy.36), channel_id=1, source_target_pairs={{0,4},{4,8},{8,12},{12,16},{16,20},{20,24},{24,28},{28,0},{1,5},{5... | collective-permute-start | bytes 58088 | tf_op jit(solution)/shard_map/ppermute | solution.py:16
  30.6 6.2 %collective-permute-start.4 = (f32[5,4,242,1]{2,1,3,0:T(4,128)}, f32[5,4,242,1]{2,1,3,0:T(4,128)}, u32[]{:S(2)}, u32[]{:S(2)}) collective-permute-start(f32[5,4,242,1]{2,1,3,0:T(4,128)} %copy.37), channel_id=1, source_target_pairs={{4,0},{8,4},{12,8},{16,12},{20,16},{24,20},{28,24},{0,28},{5,1},{9... | collective-permute-start | bytes 58088 | tf_op jit(solution)/shard_map/ppermute | solution.py:19
  53.7 1.2 %copy-start.2 = (f32[4,240,256]{2,1,0:T(8,128)S(1)}, f32[4,240,256]{2,1,0:T(8,128)}, u32[]{:S(2)}) copy-start(f32[4,240,256]{2,1,0:T(8,128)} %param.14) | copy-start | bytes 2949124
  53.7 1.5 %copy-start.3 = (f32[4,240,256]{2,1,0:T(8,128)S(1)}, f32[4,240,256]{2,1,0:T(8,128)}, u32[]{:S(2)}) copy-start(f32[4,240,256]{2,1,0:T(8,128)} %param.8) | copy-start | bytes 2949124
  53.7 1.8 %copy-start.4 = (f32[4,240,256]{2,1,0:T(8,128)S(1)}, f32[4,240,256]{2,1,0:T(8,128)}, u32[]{:S(2)}) copy-start(f32[4,240,256]{2,1,0:T(8,128)} %param.15) | copy-start | bytes 2949124
  53.7 2.1 %copy-start.9 = (f32[4,240,256]{2,1,0:T(8,128)S(1)}, f32[4,240,256]{2,1,0:T(8,128)}, u32[]{:S(2)}) copy-start(f32[4,240,256]{2,1,0:T(8,128)} %param.11) | copy-start | bytes 2949124
  53.7 2.1 %copy-start.10 = (f32[240]{0:T(256)S(1)}, f32[240]{0:T(256)}, u32[]{:S(2)}) copy-start(f32[240]{0:T(256)} %get-tuple-element.33) | copy-start | bytes 2884
  53.7 2.0 %copy-start.11 = (f32[240]{0:T(256)S(1)}, f32[240]{0:T(256)}, u32[]{:S(2)}) copy-start(f32[240]{0:T(256)} %get-tuple-element.34) | copy-start | bytes 2884
  64.9 7.1 %collective-permute-start.5 = (f32[2,1,4,1,256]{4,2,3,1,0:T(4,128)S(1)}, f32[2,1,4,1,256]{4,2,3,1,0:T(4,128)S(1)}, u32[]{:S(2)}, u32[]{:S(2)}) collective-permute-start(f32[2,1,4,1,256]{4,2,3,1,0:T(4,128)S(1)} %pad_maximum_fusion.4), channel_id=1, source_target_pairs={{16,0},{20,4},{24,8},{28,12},{0,16},{4,20},{8,24},{12,28},{17,1},{... | collective-permute-start | bytes 24584 | tf_op jit(solution)/shard_map/ppermute | solution.py:27
  65.0 5.2 %collective-permute-start.6 = (f32[1,4,1,256]{3,1,2,0:T(4,128)S(1)}, f32[1,4,1,256]{3,1,2,0:T(4,128)S(1)}, u32[]{:S(2)}, u32[]{:S(2)}) collective-permute-start(f32[1,4,1,256]{3,1,2,0:T(4,128)S(1)} %get-tuple-element.25), channel_id=1, source_target_pairs={{0,1},{1,2},{2,3},{4,5},{5,6},{6,7},{8,9},{9,10},{10,11},{12,13},{... | collective-permute-start | bytes 12296 | tf_op jit(solution)/shard_map/ppermute | solution.py:16
  68.9 3.1 %collective-permute-start.7 = (f32[1,4,1,256]{3,1,2,0:T(4,128)S(1)}, f32[1,4,1,256]{3,1,2,0:T(4,128)S(1)}, u32[]{:S(2)}, u32[]{:S(2)}) collective-permute-start(f32[1,4,1,256]{3,1,2,0:T(4,128)S(1)} %get-tuple-element.28), channel_id=1, source_target_pairs={{1,0},{2,1},{3,2},{5,4},{6,5},{7,6},{9,8},{10,9},{11,10},{13,12},{... | collective-permute-start | bytes 12296 | tf_op jit(solution)/shard_map/ppermute | solution.py:19
  72.6 21.6 %collective-permute-start.8 = (f32[1,4,242,1]{3,1,2,0:T(4,128)S(1)}, f32[1,4,242,1]{3,1,2,0:T(4,128)S(1)}, u32[]{:S(2)}, u32[]{:S(2)}) collective-permute-start(f32[1,4,242,1]{3,1,2,0:T(4,128)S(1)} %get-tuple-element.23), channel_id=1, source_target_pairs={{0,4},{4,8},{8,12},{12,16},{16,20},{20,24},{24,28},{28,0},{1,5},{5... | collective-permute-start | bytes 11624 | tf_op jit(solution)/shard_map/ppermute | solution.py:16
  73.3 23.7 %collective-permute-start.9 = (f32[1,4,242,1]{3,1,2,0:T(4,128)S(1)}, f32[1,4,242,1]{3,1,2,0:T(4,128)S(1)}, u32[]{:S(2)}, u32[]{:S(2)}) collective-permute-start(f32[1,4,242,1]{3,1,2,0:T(4,128)S(1)} %get-tuple-element.24), channel_id=1, source_target_pairs={{4,0},{8,4},{12,8},{16,12},{20,16},{24,20},{28,24},{0,28},{5,1},{9... | collective-permute-start | bytes 11624 | tf_op jit(solution)/shard_map/ppermute | solution.py:19
where the time goes:
time: 107 us; the launch traced here: 106 us
  other arithmetic  32.8 us (31%)
  local copies, waits for them, and re-layouts  27.1 us (25%)
  waiting for transfers between devices  23.6 us (22%)
  starting transfers between devices  21.6 us (20%)
    ppermute x4, waiting for transfers between devices, with_halo(): lax.ppermute(lax.slice_in_dim(block, block.shape[dim] - width, None, axis...  15.7 us
    concatenate x1, other arithmetic, with_halo(): block = jnp.concatenate([low, block, high], axis=dim)  13 us
    unnamed x31, local copies, waits for them, and re-layouts  10 us
    ppermute x4, starting transfers between devices, with_halo(): lax.ppermute(lax.slice_in_dim(block, 0, width, axis=dim), axis, backward)  9.9 us
    add x1, other arithmetic, per_device(): new_pressure = pressure + (rhs_field - applied) / diag_total  9.08 us
    ppermute x4, waiting for transfers between devices, with_halo(): lax.ppermute(lax.slice_in_dim(block, 0, width, axis=dim), axis, backward)  7.88 us
    ppermute x4, starting transfers between devices, with_halo(): lax.ppermute(lax.slice_in_dim(block, block.shape[dim] - width, None, axis...  7.55 us
    sub x1, other arithmetic, per_device(): return (new_pressure, rhs_field - applied_new)  5.77 us
  transfers between devices with their start and end apart: 10, of which 4 were waited for; matrix products, arithmetic and copies ran while one was open for 6% of the time, Pallas kernels for 0%

commit v1 on v0

v1 whole, which is shorter than its diff:
```python
import functools
import math

import jax
import jax.numpy as jnp
from jax import lax
from jax.experimental import pallas as pl
from jax.experimental.pallas import tpu as pltpu
from jax.sharding import PartitionSpec as P

LANES = 128
SUB = 8
MESH = pl.DeviceIdType.MESH


def kernel(
    lon_n, lat_n, lat_total,
    p_in, we_in, wn_in, f_in, cl_in, ct_in, cv_in, dg_in,
    np_out, res_out,
    pb, web, wnb, fb, clb, ctb, cvb, dgb,
    npb, rhsb, wwb, web2, swb, cosb,
    pk, hc, col_send, col_recv, row_send, row_recv,
    col2_send, col2_recv, row2_send, row2_recv,
    in_sem, out_sem, send_sem, recv_sem,
):
    levels, tiles, rows = web.shape[0], web.shape[1], web.shape[2]
    blocks = pk.shape[0] // LANES
    chunks = rows // SUB
    lon = lax.axis_index("lon")
    lat = lax.axis_index("lat")
    east = (lat_id(lon + 1, lon_n), lat)
    west = (lat_id(lon + lon_n - 1, lon_n), lat)
    across = lat_id(lon + lon_n // 2, lon_n)
    at_south = jnp.int32(lat == 0)
    at_north = jnp.int32(lat == lat_n - 1)
    south = (lon + at_south * (across - lon), lat - 1 + at_south)
    north = (lon + at_north * (across - lon), lat + 1 - at_north)
    partners = (west, east, south, north)

    loads = []
    for a, (src, dst, pad) in enumerate((
        (p_in, pb, SUB), (we_in, web, 0), (cl_in, clb, 0), (wn_in, wnb, SUB),
        (ct_in, ctb, SUB), (f_in, fb, 0), (cv_in, cvb, 0), (dg_in, dgb, 0),
    )):
        group = []
        for t in range(tiles):
            copy = pltpu.make_async_copy(
                src.at[:, :, pl.ds(t * LANES, LANES)],
                dst.at[:, t, pl.ds(pad, rows), :],
                in_sem.at[a, t],
            )
            copy.start()
            group.append(copy)
        loads.append(group)

    barrier = pltpu.get_barrier_semaphore()
    for lo, la in partners:
        pl.semaphore_signal(barrier, inc=1, device_id=(lo, la), device_id_type=MESH)

    lane = lax.broadcasted_iota(jnp.int32, (SUB, LANES), 1)
    lane4 = lax.broadcasted_iota(jnp.int32, (levels, tiles, SUB, LANES), 3)

    def cos_step(i, _):
        r = pl.multiple_of(i * SUB, SUB)
        face = lat * rows + r + lax.broadcasted_iota(jnp.int32, (SUB, LANES), 0)
        angle = face.astype(jnp.float32) * (math.pi / lat_total) - math.pi / 2
        cosb[pl.ds(r, SUB), :] = jnp.cos(angle)
        return 0

    lax.fori_loop(0, chunks + 1, cos_step, 0)

    def wait_load(*which):
        for a in which:
            for copy in loads[a]:
                copy.wait()

    def pack_columns(fields, pads, width):
        def step(i, _):
            r = pl.multiple_of(i * SUB, SUB)
            acc = jnp.zeros((SUB, LANES), jnp.float32)
            for f, (ref, pad) in enumerate(zip(fields, pads)):
                for k in range(levels):
                    n = f * levels + k
                    last = ref[k, tiles - 1, pl.ds(r + pad, SUB), :]
                    acc = jnp.where(lane == n, pltpu.roll(last, n + 1, 1), acc)
                    first = ref[k, 0, pl.ds(r + pad, SUB), :]
                    acc = jnp.where(lane == width + n, pltpu.roll(first, width + n, 1), acc)
            pk[pl.ds(r, SUB), :] = acc
            return 0

        lax.fori_loop(0, chunks, step, 0)

    def columns_to_rows(dst, width):
        for u in range(blocks):
            turned = pk[pl.ds(u * LANES, LANES), :].T
            dst[0, u] = turned[:width]
            dst[1, u] = turned[width:2 * width]

    def rows_to_columns(src, width):
        for u in range(blocks):
            both = jnp.concatenate(
                (src[0, u], src[1, u], jnp.zeros((LANES - 2 * width, LANES), jnp.float32)), 0
            )
            hc[pl.ds(u * LANES, LANES), :] = both.T

    def send(n, src, dst, target, slot, phase):
        copy = pltpu.make_async_remote_copy(
            src_ref=src, dst_ref=dst,
            send_sem=send_sem.at[phase, n], recv_sem=recv_sem.at[phase, slot],
            device_id=target, device_id_type=MESH,
        )
        copy.start()
        return copy

    def wait_recv(dst, slot, phase):
        pltpu.make_async_remote_copy(
            src_ref=dst, dst_ref=dst,
            send_sem=send_sem.at[phase, slot], recv_sem=recv_sem.at[phase, slot],
            device_id=east, device_id_type=MESH,
        ).wait_recv()

    south_slot = 1 - at_south
    north_slot = at_north

    def send_all(cs, cr, rs, rr, phase):
        return (
            send(0, cs.at[0], cr.at[0], east, 0, phase),
            send(1, cs.at[1], cr.at[1], west, 1, phase),
            send(2, rs.at[0], rr.at[south_slot], south, 2 + south_slot, phase),
            send(3, rs.at[1], rr.at[north_slot], north, 2 + north_slot, phase),
        )

    def pack_rows(fields, dst):
        for f, ref in enumerate(fields):
            for k in range(levels):
                n = f * levels + k
                for t in range(tiles):
                    dst[0, t, n:n + 1, :] = ref[k, t, SUB:SUB + 1, :]
                    dst[1, t, n:n + 1, :] = ref[k, t, SUB + rows - 1:SUB + rows, :]

    def unpack_rows(src, fields):
        for f, ref in enumerate(fields):
            for k in range(levels):
                n = f * levels + k
                for t in range(tiles):
                    ref[k, t, SUB - 1:SUB, :] = src[0, t, n:n + 1, :]
                    ref[k, t, SUB + rows:SUB + rows + 1, :] = src[1, t, n:n + 1, :]

    if blocks * LANES > rows:
        pk[pl.ds(rows, blocks * LANES - rows), :] = jnp.zeros(
            (blocks * LANES - rows, LANES), jnp.float32
        )
    wide = col_send.shape[2]
    narrow = col2_send.shape[2]
    row_send[...] = jnp.zeros(row_send.shape, jnp.float32)
    row2_send[...] = jnp.zeros(row2_send.shape, jnp.float32)

    wait_load(0, 1, 2)
    pack_columns((pb, web, clb), (SUB, 0, 0), wide)
    columns_to_rows(col_send, wide)
    wait_load(3, 4)
    pack_rows((pb, wnb, ctb), row_send)
    pl.semaphore_wait(barrier, len(partners))
    sends = send_all(col_send, col_recv, row_send, row_recv, 0)

    wait_load(5, 6, 7)
    for slot in (2, 3):
        wait_recv(row_recv.at[slot - 2], slot, 0)
    unpack_rows(row_recv, (pb, wnb, ctb))
    for slot in (0, 1):
        wait_recv(col_recv.at[slot], slot, 0)
    rows_to_columns(col_recv, wide)

    def halo(r, first, target):
        edge = hc[pl.ds(r, SUB), :]
        return jnp.stack(
            [pltpu.roll(edge, (target - first - k) % LANES, 1) for k in range(levels)]
        )[:, None]

    def shift(x, rim, west_side):
        if west_side:
            turned = pltpu.roll(x, 1, 3)
            beside = jnp.concatenate((rim, turned[:, :-1]), 1) if tiles > 1 else rim
            return jnp.where(lane4 == 0, beside, turned)
        turned = pltpu.roll(x, LANES - 1, 3)
        beside = jnp.concatenate((turned[:, 1:], rim), 1) if tiles > 1 else rim
        return jnp.where(lane4 == LANES - 1, beside, turned)

    def vertical(p, v):
        lower = jnp.concatenate((jnp.zeros_like(p[:1]), p[:-1]), 0)
        flux = v * (p - lower)
        return flux - jnp.concatenate((flux[1:], jnp.zeros_like(p[:1])), 0)

    def first_pass(i, _):
        r = pl.multiple_of(i * SUB, SUB)
        here = pl.ds(r, SUB)
        mid, low, high = pl.ds(r + SUB, SUB), pl.ds(r + SUB - 1, SUB), pl.ds(r + SUB + 1, SUB)
        c_low = cosb[here, :]
        c_high = cosb[pl.ds(r + 1, SUB), :]
        m_low = 0.25 * (1.0 + jnp.abs(c_low))
        m_high = 0.25 * (1.0 + jnp.abs(c_high))
        we = web[:, :, here, :]
        zonal = shift(we, halo(r, wide + levels, LANES - 1), False) - shift(
            we, halo(r, levels, 0), True
        )
        wn = wnb[:, :, mid, :]
        merid = c_high * (wn + wnb[:, :, high, :]) - c_low * (wnb[:, :, low, :] + wn)
        rhs = fb[:, :, here, :] - 0.5 * (zonal + merid)
        rhsb[:, :, here, :] = rhs
        cl = clb[:, :, here, :]
        w_west = 0.5 * (cl + shift(cl, halo(r, 2 * levels, 0), True))
        w_east = 0.5 * (cl + shift(cl, halo(r, wide + 2 * levels, LANES - 1), False))
        wwb[:, :, here, :] = w_west
        web2[:, :, here, :] = w_east
        ct = ctb[:, :, mid, :]
        w_south = m_low * (ct + ctb[:, :, low, :])
        w_north = m_high * (ct + ctb[:, :, high, :])
        swb[:, :, here, :] = w_south
        swb[:, :, pl.ds(r + 1, SUB), :] = w_north
        v = cvb[:, :, here, :]
        dg = dgb[:, :, here, :]
        upper = jnp.concatenate((v[1:], jnp.zeros_like(v[:1])), 0)
        total = dg + w_west + w_east + w_south + w_north + v + upper
        p = pb[:, :, mid, :]
        applied = dg * p + vertical(p, v)
        applied += w_west * (p - shift(p, halo(r, 0, 0), True))
        applied += w_east * (p - shift(p, halo(r, wide, LANES - 1), False))
        applied += w_south * (p - pb[:, :, low, :])
        applied += w_north * (p - pb[:, :, high, :])
        npb[:, :, mid, :] = p + (rhs - applied) / total
        return 0

    lax.fori_loop(0, chunks, first_pass, 0)

    pack_columns((npb,), (SUB,), narrow)
    columns_to_rows(col2_send, narrow)
    pack_rows((npb,), row2_send)
    sends += send_all(col2_send, col2_recv, row2_send, row2_recv, 1)

    stores = []
    for t in range(tiles):
        copy = pltpu.make_async_copy(
            npb.at[:, t, pl.ds(SUB, rows), :],
            np_out.at[:, :, pl.ds(t * LANES, LANES)],
            out_sem.at[0, t],
        )
        copy.start()
        stores.append(copy)

    for slot in (2, 3):
        wait_recv(row2_recv.at[slot - 2], slot, 1)
    unpack_rows(row2_recv, (npb,))
    for slot in (0, 1):
        wait_recv(col2_recv.at[slot], slot, 1)
    rows_to_columns(col2_recv, narrow)

    def second_pass(i, _):
        r = pl.multiple_of(i * SUB, SUB)
        here = pl.ds(r, SUB)
        mid, low, high = pl.ds(r + SUB, SUB), pl.ds(r + SUB - 1, SUB), pl.ds(r + SUB + 1, SUB)
        p = npb[:, :, mid, :]
        applied = dgb[:, :, here, :] * p + vertical(p, cvb[:, :, here, :])
        applied += wwb[:, :, here, :] * (p - shift(p, halo(r, 0, 0), True))
        applied += web2[:, :, here, :] * (p - shift(p, halo(r, narrow, LANES - 1), False))
        applied += swb[:, :, here, :] * (p - npb[:, :, low, :])
        applied += swb[:, :, pl.ds(r + 1, SUB), :] * (p - npb[:, :, high, :])
        rhsb[:, :, here, :] = rhsb[:, :, here, :] - applied
        return 0

    lax.fori_loop(0, chunks, second_pass, 0)

    for t in range(tiles):
        copy = pltpu.make_async_copy(
            rhsb.at[:, t],
            res_out.at[:, :, pl.ds(t * LANES, LANES)],
            out_sem.at[1, t],
        )
        copy.start()
        stores.append(copy)
    for copy in sends:
        copy.wait_send()
    for copy in stores:
        copy.wait()


def lat_id(index, count):
    return lax.rem(index, count)


def per_device(lon_n, lat_n, *fields):
    levels, rows, width = fields[0].shape
    tiles = width // LANES
    blocks = -(-rows // LANES)
    f32 = jnp.float32
    plain = pltpu.VMEM((levels, tiles, rows, LANES), f32)
    padded = pltpu.VMEM((levels, tiles, rows + 2 * SUB, LANES), f32)
    face = pltpu.VMEM((levels, tiles, rows + SUB, LANES), f32)
    wide = -(-3 * levels // SUB) * SUB
    narrow = -(-levels // SUB) * SUB
    cols = lambda n: pltpu.VMEM((2, blocks, n, LANES), f32)
    edge = lambda n: pltpu.VMEM((2, tiles, n, LANES), f32)
    shape = jax.ShapeDtypeStruct((levels, rows, width), f32)
    any_spec = pl.BlockSpec(memory_space=pl.ANY)
    return pl.pallas_call(
        functools.partial(kernel, lon_n, lat_n, rows * lat_n),
        out_shape=(shape, shape),
        in_specs=[any_spec] * 8,
        out_specs=(any_spec, any_spec),
        scratch_shapes=[
            padded, plain, padded, plain, plain, padded, plain, plain,
            padded, plain, plain, plain, face, pltpu.VMEM((rows + 2 * SUB, LANES), f32),
            pltpu.VMEM((blocks * LANES, LANES), f32), pltpu.VMEM((blocks * LANES, LANES), f32),
            cols(wide), cols(wide), edge(wide), edge(wide),
            cols(narrow), cols(narrow), edge(narrow), edge(narrow),
            pltpu.SemaphoreType.DMA((8, tiles)),
            pltpu.SemaphoreType.DMA((2, tiles)),
            pltpu.SemaphoreType.DMA((2, 4)),
            pltpu.SemaphoreType.DMA((2, 4)),
        ],
        compiler_params=pltpu.CompilerParams(
            collective_id=0, has_side_effects=True, vmem_limit_bytes=48 * 1024 * 1024
        ),
    )(*fields)


def solution(mesh):
    spec = P(None, "lat", "lon")
    return jax.shard_map(
        functools.partial(per_device, mesh.shape["lon"], mesh.shape["lat"]),
        mesh=mesh, in_specs=(spec,) * 8, out_specs=(spec, spec), check_vma=False,
    )
```

time: 107 us -> 33.3 us (0.31)
  other arithmetic: 32.8 us -> 0 us
  Pallas kernels: 0 us -> 25.6 us
  waiting for transfers between devices: 23.6 us -> 0 us
  starting transfers between devices: 21.6 us -> 0 us
  local copies, waits for them, and re-layouts: 27.1 us -> 6.69 us
    pallas_call x0 -> x1, Pallas kernels: none -> 25.6 us  [per_device(): pl.pallas_call(functools.partial(kernel, lon_n, lat_n, rows * lat_n), out...]
    ppermute x10 -> x0, waiting for transfers between devices: 23.6 us -> none  [the longest x4 15.7 us: with_halo(): lax.ppermute(lax.slice_in_dim(block, block.shape[dim] - width, None, axis...]
    ppermute x10 -> x0, starting transfers between devices: 21.6 us -> none  [the longest x4 9.9 us: with_halo(): lax.ppermute(lax.slice_in_dim(block, 0, width, axis=dim), axis, backward)]
    concatenate x3 -> x0, other arithmetic: 16.7 us -> none  [the longest x1 13 us: with_halo(): block = jnp.concatenate([low, block, high], axis=dim)]
    slice x10 -> x0, local copies, waits for them, and re-layouts: 10.7 us -> none  [the longest x3 5.64 us: with_halo(): lax.slice_in_dim(block, block.shape[dim] - width, None, axis=dim)]
    add x1 -> x0, other arithmetic: 9.08 us -> none  [per_device(): new_pressure = pressure + (rhs_field - applied) / diag_total]
    sub x1 -> x0, other arithmetic: 5.77 us -> none  [per_device(): return (new_pressure, rhs_field - applied_new)]
    ppermute x2 -> x0, local copies, waits for them, and re-layouts: 4.33 us -> none  [the longest x1 2.59 us: with_halo(): lax.ppermute(lax.slice_in_dim(block, 0, width, axis=dim), axis, backward)]
  transfers between devices with their start and end apart: 10 -> 0, of which waited for: 4 -> 0; matrix products, arithmetic and copies ran while one was open for 6% -> 0% of each run, Pallas kernels for 0% -> 0%
where the time goes in v1:
time: 33.3 us; the launch traced here: 32.9 us
  Pallas kernels  25.6 us (77%)
  local copies, waits for them, and re-layouts  6.69 us (20%)
  between operations  0.65 us (2%)
    pallas_call x1, Pallas kernels, per_device(): pl.pallas_call(functools.partial(kernel, lon_n, lat_n, rows * lat_n), out...  25.6 us
    unnamed x10, local copies, waits for them, and re-layouts  6.69 us

profile of v1, /device:TPU:0, one launch (start us, length us, event | category | flops | bytes accessed | tf_op | source)
XLA Modules:
  0.0 32.9 jit_solution(14500272822745510523)
XLA Ops:
  0.6 0.0 copy-start
  0.6 1.2 %copy-done = f32[4,240,256]{2,1,0:T(8,128)S(1)} copy-done((f32[4,240,256]{2,1,0:T(8,128)S(1)}, f32[4,240,256]{2,1,0:T(8,128)}, u32[]{:S(2)}) %copy-start) | copy-done | bytes 983064
  1.8 0.0 copy-start.1
  1.8 1.2 %copy-done.1 = f32[4,240,256]{2,1,0:T(8,128)S(1)} copy-done((f32[4,240,256]{2,1,0:T(8,128)S(1)}, f32[4,240,256]{2,1,0:T(8,128)}, u32[]{:S(2)}) %copy-start.1) | copy-done | bytes 983064
  3.0 0.0 copy-start.2
  3.0 1.2 %copy-done.2 = f32[4,240,256]{2,1,0:T(8,128)S(1)} copy-done((f32[4,240,256]{2,1,0:T(8,128)S(1)}, f32[4,240,256]{2,1,0:T(8,128)}, u32[]{:S(2)}) %copy-start.2) | copy-done | bytes 983064
  4.2 0.0 copy-start.3
  4.2 1.2 %copy-done.3 = f32[4,240,256]{2,1,0:T(8,128)S(1)} copy-done((f32[4,240,256]{2,1,0:T(8,128)S(1)}, f32[4,240,256]{2,1,0:T(8,128)}, u32[]{:S(2)}) %copy-start.3) | copy-done | bytes 983064
  5.4 25.6 %shard_map.95 = (f32[4,240,256]{2,1,0:T(8,128)S(1)}, f32[4,240,256]{2,1,0:T(8,128)S(1)}) custom-call(f32[4,240,256]{2,1,0:T(8,128)S(1)} %copy-done, f32[4,240,256]{2,1,0:T(8,128)S(1)} %copy-done.1, f32[4,240,256]{2,1,0:T(8,128)S(1)} %copy-done.2, f32[4,240,256]{2,1,0:T(8,128)S(1)} %copy-done.3, f32[4,240,256]{2,1,0:T(8,128)} %cl_in.1, f32[4,240,256]{2,1,0:T(8,128)} %ct_in.1, ...), custom_call_target="tpu_custom_call" | custom-call | tf_op jit(solution)/shard_map/pallas_call | solution.py:304
  31.0 0.9 %copy.12 = f32[4,240,256]{2,1,0:T(8,128)} copy(f32[4,240,256]{2,1,0:T(8,128)S(1)} %get-tuple-element.4) | data formatting | bytes 1966080
  32.0 0.9 %copy.13 = f32[4,240,256]{2,1,0:T(8,128)} copy(f32[4,240,256]{2,1,0:T(8,128)S(1)} %get-tuple-element.5) | data formatting | bytes 1966080
Async XLA Ops:
  0.6 1.2 %copy-start = (f32[4,240,256]{2,1,0:T(8,128)S(1)}, f32[4,240,256]{2,1,0:T(8,128)}, u32[]{:S(2)}) copy-start(f32[4,240,256]{2,1,0:T(8,128)} %p_in.1) | copy-start | bytes 2949124
  1.8 1.2 %copy-start.1 = (f32[4,240,256]{2,1,0:T(8,128)S(1)}, f32[4,240,256]{2,1,0:T(8,128)}, u32[]{:S(2)}) copy-start(f32[4,240,256]{2,1,0:T(8,128)} %we_in.1) | copy-start | bytes 2949124
  3.0 1.2 %copy-start.2 = (f32[4,240,256]{2,1,0:T(8,128)S(1)}, f32[4,240,256]{2,1,0:T(8,128)}, u32[]{:S(2)}) copy-start(f32[4,240,256]{2,1,0:T(8,128)} %wn_in.1) | copy-start | bytes 2949124
  4.2 1.2 %copy-start.3 = (f32[4,240,256]{2,1,0:T(8,128)S(1)}, f32[4,240,256]{2,1,0:T(8,128)}, u32[]{:S(2)}) copy-start(f32[4,240,256]{2,1,0:T(8,128)} %f_in.1) | copy-start | bytes 2949124

commit v2 on v1

--- a/solution.py
+++ b/solution.py
@@ -18,7 +18,7 @@
     p_in, we_in, wn_in, f_in, cl_in, ct_in, cv_in, dg_in,
     np_out, res_out,
     pb, web, wnb, fb, clb, ctb, cvb, dgb,
-    npb, rhsb, wwb, web2, swb, cosb,
+    npb, rhsb, rhs2b, appb, totb, accb, resb, wwb, ewb, swb, nwb, cosb,
     pk, hc, col_send, col_recv, row_send, row_recv,
     col2_send, col2_recv, row2_send, row2_recv,
     in_sem, out_sem, send_sem, recv_sem,
@@ -60,35 +60,34 @@
     lane = lax.broadcasted_iota(jnp.int32, (SUB, LANES), 1)
     lane4 = lax.broadcasted_iota(jnp.int32, (levels, tiles, SUB, LANES), 3)
 
-    def cos_step(i, _):
-        r = pl.multiple_of(i * SUB, SUB)
-        face = lat * rows + r + lax.broadcasted_iota(jnp.int32, (SUB, LANES), 0)
-        angle = face.astype(jnp.float32) * (math.pi / lat_total) - math.pi / 2
-        cosb[pl.ds(r, SUB), :] = jnp.cos(angle)
-        return 0
-
-    lax.fori_loop(0, chunks + 1, cos_step, 0)
+    face = lat * rows + lax.broadcasted_iota(jnp.int32, cosb.shape, 0)
+    cosb[...] = jnp.cos(face.astype(jnp.float32) * (math.pi / lat_total) - math.pi / 2)
 
     def wait_load(*which):
         for a in which:
             for copy in loads[a]:
                 copy.wait()
 
-    def pack_columns(fields, pads, width):
-        def step(i, _):
-            r = pl.multiple_of(i * SUB, SUB)
-            acc = jnp.zeros((SUB, LANES), jnp.float32)
-            for f, (ref, pad) in enumerate(zip(fields, pads)):
-                for k in range(levels):
-                    n = f * levels + k
-                    last = ref[k, tiles - 1, pl.ds(r + pad, SUB), :]
-                    acc = jnp.where(lane == n, pltpu.roll(last, n + 1, 1), acc)
-                    first = ref[k, 0, pl.ds(r + pad, SUB), :]
-                    acc = jnp.where(lane == width + n, pltpu.roll(first, width + n, 1), acc)
-            pk[pl.ds(r, SUB), :] = acc
-            return 0
-
-        lax.fori_loop(0, chunks, step, 0)
+    def loop(first, last, step):
+        size = max(n for n in range(1, 6) if (last - first) % n == 0)
+        lax.fori_loop(first, last, step, 0, unroll=size)
+
+    def packed(fields, width):
+        acc = jnp.zeros((SUB, LANES), jnp.float32)
+        for f, field in enumerate(fields):
+            for k in range(levels):
+                n = f * levels + k
+                acc = jnp.where(lane == n, pltpu.roll(field[k, tiles - 1], n + 1, 1), acc)
+                acc = jnp.where(lane == width + n, pltpu.roll(field[k, 0], width + n, 1), acc)
+        return acc
+
+    def pack_first(i, _):
+        r = pl.multiple_of(i * SUB, SUB)
+        here = pl.ds(r, SUB)
+        pk[here, :] = packed(
+            [pb[:, :, pl.ds(r + SUB, SUB), :], web[:, :, here, :], clb[:, :, here, :]], wide
+        )
+        return 0
 
     def columns_to_rows(dst, width):
         for u in range(blocks):
@@ -156,7 +155,7 @@
     row2_send[...] = jnp.zeros(row2_send.shape, jnp.float32)
 
     wait_load(0, 1, 2)
-    pack_columns((pb, web, clb), (SUB, 0, 0), wide)
+    loop(0, chunks, pack_first)
     columns_to_rows(col_send, wide)
     wait_load(3, 4)
     pack_rows((pb, wnb, ctb), row_send)
@@ -164,12 +163,6 @@
     sends = send_all(col_send, col_recv, row_send, row_recv, 0)
 
     wait_load(5, 6, 7)
-    for slot in (2, 3):
-        wait_recv(row_recv.at[slot - 2], slot, 0)
-    unpack_rows(row_recv, (pb, wnb, ctb))
-    for slot in (0, 1):
-        wait_recv(col_recv.at[slot], slot, 0)
-    rows_to_columns(col_recv, wide)
 
     def halo(r, first, target):
         edge = hc[pl.ds(r, SUB), :]
@@ -191,92 +184,110 @@
         flux = v * (p - lower)
         return flux - jnp.concatenate((flux[1:], jnp.zeros_like(p[:1])), 0)
 
-    def first_pass(i, _):
+    def slices(i):
         r = pl.multiple_of(i * SUB, SUB)
-        here = pl.ds(r, SUB)
-        mid, low, high = pl.ds(r + SUB, SUB), pl.ds(r + SUB - 1, SUB), pl.ds(r + SUB + 1, SUB)
+        return r, pl.ds(r, SUB), pl.ds(r + SUB, SUB), pl.ds(r + SUB - 1, SUB), pl.ds(r + SUB + 1, SUB)
+
+    def first_inner(i, _):
+        r, here, mid, low, high = slices(i)
         c_low = cosb[here, :]
         c_high = cosb[pl.ds(r + 1, SUB), :]
         m_low = 0.25 * (1.0 + jnp.abs(c_low))
         m_high = 0.25 * (1.0 + jnp.abs(c_high))
+        wn = wnb[:, :, mid, :]
+        merid = c_high * (wn + wnb[:, :, high, :]) - c_low * (wnb[:, :, low, :] + wn)
+        rhsb[:, :, here, :] = fb[:, :, here, :] - 0.5 * merid
+        ct = ctb[:, :, mid, :]
+        w_south = m_low * (ct + ctb[:, :, low, :])
+        w_north = m_high * (ct + ctb[:, :, high, :])
+        swb[:, :, here, :] = w_south
+        nwb[:, :, here, :] = w_north
+        v = cvb[:, :, here, :]
+        dg = dgb[:, :, here, :]
+        upper = jnp.concatenate((v[1:], jnp.zeros_like(v[:1])), 0)
+        totb[:, :, here, :] = dg + w_south + w_north + v + upper
+        p = pb[:, :, mid, :]
+        applied = dg * p + vertical(p, v)
+        applied += w_south * (p - pb[:, :, low, :])
+        appb[:, :, here, :] = applied + w_north * (p - pb[:, :, high, :])
+        return 0
+
+    def first_outer(i, _):
+        r, here, mid, low, high = slices(i)
         we = web[:, :, here, :]
         zonal = shift(we, halo(r, wide + levels, LANES - 1), False) - shift(
             we, halo(r, levels, 0), True
         )
-        wn = wnb[:, :, mid, :]
-        merid = c_high * (wn + wnb[:, :, high, :]) - c_low * (wnb[:, :, low, :] + wn)
-        rhs = fb[:, :, here, :] - 0.5 * (zonal + merid)
-        rhsb[:, :, here, :] = rhs
+        rhs = rhsb[:, :, here, :] - 0.5 * zonal
+        rhs2b[:, :, here, :] = rhs
         cl = clb[:, :, here, :]
         w_west = 0.5 * (cl + shift(cl, halo(r, 2 * levels, 0), True))
         w_east = 0.5 * (cl + shift(cl, halo(r, wide + 2 * levels, LANES - 1), False))
         wwb[:, :, here, :] = w_west
-        web2[:, :, here, :] = w_east
-        ct = ctb[:, :, mid, :]
-        w_south = m_low * (ct + ctb[:, :, low, :])
-        w_north = m_high * (ct + ctb[:, :, high, :])
-        swb[:, :, here, :] = w_south
-        swb[:, :, pl.ds(r + 1, SUB), :] = w_north
-        v = cvb[:, :, here, :]
-        dg = dgb[:, :, here, :]
-        upper = jnp.concatenate((v[1:], jnp.zeros_like(v[:1])), 0)
-        total = dg + w_west + w_east + w_south + w_north + v + upper
+        ewb[:, :, here, :] = w_east
+        total = totb[:, :, here, :] + w_west + w_east
         p = pb[:, :, mid, :]
-        applied = dg * p + vertical(p, v)
+        applied = appb[:, :, here, :]
         applied += w_west * (p - shift(p, halo(r, 0, 0), True))
         applied += w_east * (p - shift(p, halo(r, wide, LANES - 1), False))
-        applied += w_south * (p - pb[:, :, low, :])
-        applied += w_north * (p - pb[:, :, high, :])
-        npb[:, :, mid, :] = p + (rhs - applied) / total
-        return 0
-
-    lax.fori_loop(0, chunks, first_pass, 0)
-
-    pack_columns((npb,), (SUB,), narrow)
+        fresh = p + (rhs - applied) / total
+        npb[:, :, mid, :] = fresh
+        pk[here, :] = packed([fresh], narrow)
+        return 0
+
+    def second_inner(i, _):
+        r, here, mid, low, high = slices(i)
+        p = npb[:, :, mid, :]
+        applied = dgb[:, :, here, :] * p + vertical(p, cvb[:, :, here, :])
+        applied += swb[:, :, here, :] * (p - npb[:, :, low, :])
+        applied += nwb[:, :, here, :] * (p - npb[:, :, high, :])
+        accb[:, :, here, :] = rhs2b[:, :, here, :] - applied
+        return 0
+
+    def second_outer(i, _):
+        r, here, mid, low, high = slices(i)
+        p = npb[:, :, mid, :]
+        acc = accb[:, :, here, :]
+        acc -= wwb[:, :, here, :] * (p - shift(p, halo(r, 0, 0), True))
+        acc -= ewb[:, :, here, :] * (p - shift(p, halo(r, narrow, LANES - 1), False))
+        resb[:, :, here, :] = acc
+        return 0
+
+    def inner_rows(step, src, fields, phase):
+        loop(1, chunks - 1, step)
+        for slot in (2, 3):
+            wait_recv(src.at[slot - 2], slot, phase)
+        unpack_rows(src, fields)
+        step(0, 0)
+        step(chunks - 1, 0)
+
+    inner_rows(first_inner, row_recv, (pb, wnb, ctb), 0)
+    for slot in (0, 1):
+        wait_recv(col_recv.at[slot], slot, 0)
+    rows_to_columns(col_recv, wide)
+    loop(0, chunks, first_outer)
+
     columns_to_rows(col2_send, narrow)
     pack_rows((npb,), row2_send)
     sends += send_all(col2_send, col2_recv, row2_send, row2_recv, 1)
 
     stores = []
-    for t in range(tiles):
-        copy = pltpu.make_async_copy(
-            npb.at[:, t, pl.ds(SUB, rows), :],
-            np_out.at[:, :, pl.ds(t * LANES, LANES)],
-            out_sem.at[0, t],
-        )
-        copy.start()
-        stores.append(copy)
-
-    for slot in (2, 3):
-        wait_recv(row2_recv.at[slot - 2], slot, 1)
-    unpack_rows(row2_recv, (npb,))
+
+    def store(n, src, dst):
+        for t in range(tiles):
+            copy = pltpu.make_async_copy(
+                src(t), dst.at[:, :, pl.ds(t * LANES, LANES)], out_sem.at[n, t]
+            )
+            copy.start()
+            stores.append(copy)
+
+    store(0, lambda t: npb.at[:, t, pl.ds(SUB, rows), :], np_out)
+    inner_rows(second_inner, row2_recv, (npb,), 1)
     for slot in (0, 1):
         wait_recv(col2_recv.at[slot], slot, 1)
     rows_to_columns(col2_recv, narrow)
-
-    def second_pass(i, _):
-        r = pl.multiple_of(i * SUB, SUB)
-        here = pl.ds(r, SUB)
-        mid, low, high = pl.ds(r + SUB, SUB), pl.ds(r + SUB - 1, SUB), pl.ds(r + SUB + 1, SUB)
-        p = npb[:, :, mid, :]
-        applied = dgb[:, :, here, :] * p + vertical(p, cvb[:, :, here, :])
-        applied += wwb[:, :, here, :] * (p - shift(p, halo(r, 0, 0), True))
-        applied += web2[:, :, here, :] * (p - shift(p, halo(r, narrow, LANES - 1), False))
-        applied += swb[:, :, here, :] * (p - npb[:, :, low, :])
-        applied += swb[:, :, pl.ds(r + 1, SUB), :] * (p - npb[:, :, high, :])
-        rhsb[:, :, here, :] = rhsb[:, :, here, :] - applied
-        return 0
-
-    lax.fori_loop(0, chunks, second_pass, 0)
-
-    for t in range(tiles):
-        copy = pltpu.make_async_copy(
-            rhsb.at[:, t],
-            res_out.at[:, :, pl.ds(t * LANES, LANES)],
-            out_sem.at[1, t],
-        )
-        copy.start()
-        stores.append(copy)
+    loop(0, chunks, second_outer)
+    store(1, lambda t: resb.at[:, t], res_out)
     for copy in sends:
         copy.wait_send()
     for copy in stores:
@@ -294,7 +305,6 @@
     f32 = jnp.float32
     plain = pltpu.VMEM((levels, tiles, rows, LANES), f32)
     padded = pltpu.VMEM((levels, tiles, rows + 2 * SUB, LANES), f32)
-    face = pltpu.VMEM((levels, tiles, rows + SUB, LANES), f32)
     wide = -(-3 * levels // SUB) * SUB
     narrow = -(-levels // SUB) * SUB
     cols = lambda n: pltpu.VMEM((2, blocks, n, LANES), f32)
@@ -308,7 +318,7 @@
         out_specs=(any_spec, any_spec),
         scratch_shapes=[
             padded, plain, padded, plain, plain, padded, plain, plain,
-            padded, plain, plain, plain, face, pltpu.VMEM((rows + 2 * SUB, LANES), f32),
+            padded] + [plain] * 10 + [pltpu.VMEM((rows + SUB, LANES), f32),
             pltpu.VMEM((blocks * LANES, LANES), f32), pltpu.VMEM((blocks * LANES, LANES), f32),
             cols(wide), cols(wide), edge(wide), edge(wide),
             cols(narrow), cols(narrow), edge(narrow), edge(narrow),
@@ -320,7 +330,7 @@
         compiler_params=pltpu.CompilerParams(
             collective_id=0, has_side_effects=True, vmem_limit_bytes=48 * 1024 * 1024
         ),
-    )(*fields)
+    )(*(pltpu.with_memory_space_constraint(x, pltpu.HBM) for x in fields))
 
 
 def solution(mesh):

time: 33.3 us -> 23.6 us (0.71)
  local copies, waits for them, and re-layouts: 6.69 us -> 1.89 us
  Pallas kernels: 25.6 us -> 20.9 us
    unnamed x10 -> x2, local copies, waits for them, and re-layouts: 6.69 us -> 1.89 us
    pallas_call x1, Pallas kernels: 25.6 us -> 20.9 us  [per_device(): pl.pallas_call(functools.partial(kernel, lon_n, lat_n, rows * lat_n), out...]
where the time goes in v2:
time: 23.6 us; the launch traced here: 23.5 us
  Pallas kernels  20.9 us (89%)
  local copies, waits for them, and re-layouts  1.89 us (8%)
  between operations  0.64 us (3%)
    pallas_call x1, Pallas kernels, per_device(): pl.pallas_call(functools.partial(kernel, lon_n, lat_n, rows * lat_n), out...  20.9 us
    unnamed x2, local copies, waits for them, and re-layouts  1.89 us

profile of v2, /device:TPU:0, one launch (start us, length us, event | category | flops | bytes accessed | tf_op | source)
XLA Modules:
  0.0 23.5 jit_solution(15565330215079891074)
XLA Ops:
  0.6 20.9 %shard_map.95 = (f32[4,240,256]{2,1,0:T(8,128)S(1)}, f32[4,240,256]{2,1,0:T(8,128)S(1)}) custom-call(f32[4,240,256]{2,1,0:T(8,128)} %p_in.1, f32[4,240,256]{2,1,0:T(8,128)} %we_in.1, f32[4,240,256]{2,1,0:T(8,128)} %wn_in.1, f32[4,240,256]{2,1,0:T(8,128)} %f_in.1, f32[4,240,256]{2,1,0:T(8,128)} %cl_in.1, f32[4,240,256]{2,1,0:T(8,128)} %ct_in.1, ...), custom_call_target="tpu_custom_call" | custom-call | tf_op jit(solution)/shard_map/pallas_call | solution.py:314
  21.6 0.9 %copy.12 = f32[4,240,256]{2,1,0:T(8,128)} copy(f32[4,240,256]{2,1,0:T(8,128)S(1)} %get-tuple-element.4) | data formatting | bytes 1966080
  22.5 0.9 %copy.13 = f32[4,240,256]{2,1,0:T(8,128)} copy(f32[4,240,256]{2,1,0:T(8,128)S(1)} %get-tuple-element.5) | data formatting | bytes 1966080

commit v3 on v2

--- a/solution.py
+++ b/solution.py
@@ -13,15 +13,87 @@
 MESH = pl.DeviceIdType.MESH
 
 
+def loop(first, last, step):
+    size = max(n for n in range(1, 6) if (last - first) % n == 0)
+    lax.fori_loop(first, last, step, 0, unroll=size)
+
+
+def slices(i):
+    r = pl.multiple_of(i * SUB, SUB)
+    return r, pl.ds(r, SUB), pl.ds(r + SUB, SUB), pl.ds(r + SUB - 1, SUB), pl.ds(r + SUB + 1, SUB)
+
+
+def halo(hc, levels, r, first, target):
+    edge = hc[pl.ds(r, SUB), :]
+    return jnp.stack(
+        [pltpu.roll(edge, (target - first - k) % LANES, 1) for k in range(levels)]
+    )[:, None]
+
+
+def shift(x, rim, west_side):
+    tiles = x.shape[1]
+    lane4 = lax.broadcasted_iota(jnp.int32, x.shape, 3)
+    if west_side:
+        turned = pltpu.roll(x, 1, 3)
+        beside = jnp.concatenate((rim, turned[:, :-1]), 1) if tiles > 1 else rim
+        return jnp.where(lane4 == 0, beside, turned)
+    turned = pltpu.roll(x, LANES - 1, 3)
+    beside = jnp.concatenate((turned[:, 1:], rim), 1) if tiles > 1 else rim
+    return jnp.where(lane4 == LANES - 1, beside, turned)
+
+
+def vertical(p, v):
+    lower = jnp.concatenate((jnp.zeros_like(p[:1]), p[:-1]), 0)
+    flux = v * (p - lower)
+    return flux - jnp.concatenate((flux[1:], jnp.zeros_like(p[:1])), 0)
+
+
+def finish(narrow, npb, accb, wwb, ewb, hc, np_out, res_out, resb, sem):
+    levels, tiles, rows = accb.shape[0], accb.shape[1], accb.shape[2]
+    chunks = rows // SUB
+    parts = max(n for n in range(1, 4) if chunks % n == 0)
+    span = rows // parts
+    copies = []
+
+    def store(n, part, src, pad, dst):
+        for t in range(tiles):
+            copy = pltpu.make_async_copy(
+                src.at[:, t, pl.ds(part * span + pad, span), :],
+                dst.at[:, pl.ds(part * span, span), pl.ds(t * LANES, LANES)],
+                sem.at[n, part, t],
+            )
+            copy.start()
+            copies.append(copy)
+
+    def step(i, _):
+        r, here, mid, low, high = slices(i)
+        p = npb[:, :, mid, :]
+        acc = accb[:, :, here, :]
+        acc -= wwb[:, :, here, :] * (p - shift(p, halo(hc, levels, r, 0, 0), True))
+        acc -= ewb[:, :, here, :] * (
+            p - shift(p, halo(hc, levels, r, narrow, LANES - 1), False)
+        )
+        resb[:, :, here, :] = acc
+        return 0
+
+    for part in range(parts):
+        store(0, part, npb, SUB, np_out)
+    for part in range(parts):
+        loop(part * (chunks // parts), (part + 1) * (chunks // parts), step)
+        store(1, part, resb, 0, res_out)
+    for copy in copies:
+        copy.wait()
+
+
 def kernel(
     lon_n, lat_n, lat_total,
     p_in, we_in, wn_in, f_in, cl_in, ct_in, cv_in, dg_in,
-    np_out, res_out,
+    npb, accb, wwb, ewb, hc,
     pb, web, wnb, fb, clb, ctb, cvb, dgb,
-    npb, rhsb, rhs2b, appb, totb, accb, resb, wwb, ewb, swb, nwb, cosb,
-    pk, hc, col_send, col_recv, row_send, row_recv,
+    rhsb, rhs2b, appb, totb, swb, nwb, cosb,
+    pk, col_send, col_recv, row_send, row_recv,
     col2_send, col2_recv, row2_send, row2_recv,
-    in_sem, out_sem, send_sem, recv_sem,
+    in_sem, send_sem, recv_sem,
 ):
     levels, tiles, rows = web.shape[0], web.shape[1], web.shape[2]
     blocks = pk.shape[0] // LANES
@@ -49,16 +121,21 @@
                 dst.at[:, t, pl.ds(pad, rows), :],
                 in_sem.at[a, t],
             )
-            copy.start()
             group.append(copy)
         loads.append(group)
+
+    def start_load(*which):
+        for a in which:
+            for copy in loads[a]:
+                copy.start()
+
+    start_load(0, 1, 2, 3, 4)
 
     barrier = pltpu.get_barrier_semaphore()
     for lo, la in partners:
         pl.semaphore_signal(barrier, inc=1, device_id=(lo, la), device_id_type=MESH)
 
     lane = lax.broadcasted_iota(jnp.int32, (SUB, LANES), 1)
-    lane4 = lax.broadcasted_iota(jnp.int32, (levels, tiles, SUB, LANES), 3)
 
     face = lat * rows + lax.broadcasted_iota(jnp.int32, cosb.shape, 0)
     cosb[...] = jnp.cos(face.astype(jnp.float32) * (math.pi / lat_total) - math.pi / 2)
@@ -67,10 +144,6 @@
         for a in which:
             for copy in loads[a]:
                 copy.wait()
-
-    def loop(first, last, step):
-        size = max(n for n in range(1, 6) if (last - first) % n == 0)
-        lax.fori_loop(first, last, step, 0, unroll=size)
 
     def packed(fields, width):
         acc = jnp.zeros((SUB, LANES), jnp.float32)
@@ -155,6 +228,7 @@
     row2_send[...] = jnp.zeros(row2_send.shape, jnp.float32)
 
     wait_load(0, 1, 2)
+    start_load(5, 6, 7)
     loop(0, chunks, pack_first)
     columns_to_rows(col_send, wide)
     wait_load(3, 4)
@@ -163,30 +237,6 @@
     sends = send_all(col_send, col_recv, row_send, row_recv, 0)
 
     wait_load(5, 6, 7)
-
-    def halo(r, first, target):
-        edge = hc[pl.ds(r, SUB), :]
-        return jnp.stack(
-            [pltpu.roll(edge, (target - first - k) % LANES, 1) for k in range(levels)]
-        )[:, None]
-
-    def shift(x, rim, west_side):
-        if west_side:
-            turned = pltpu.roll(x, 1, 3)
-            beside = jnp.concatenate((rim, turned[:, :-1]), 1) if tiles > 1 else rim
-            return jnp.where(lane4 == 0, beside, turned)
-        turned = pltpu.roll(x, LANES - 1, 3)
-        beside = jnp.concatenate((turned[:, 1:], rim), 1) if tiles > 1 else rim
-        return jnp.where(lane4 == LANES - 1, beside, turned)
-
-    def vertical(p, v):
-        lower = jnp.concatenate((jnp.zeros_like(p[:1]), p[:-1]), 0)
-        flux = v * (p - lower)
-        return flux - jnp.concatenate((flux[1:], jnp.zeros_like(p[:1])), 0)
-
-    def slices(i):
-        r = pl.multiple_of(i * SUB, SUB)
-        return r, pl.ds(r, SUB), pl.ds(r + SUB, SUB), pl.ds(r + SUB - 1, SUB), pl.ds(r + SUB + 1, SUB)
 
     def first_inner(i, _):
         r, here, mid, low, high = slices(i)
@@ -215,21 +265,21 @@
     def first_outer(i, _):
         r, here, mid, low, high = slices(i)
         we = web[:, :, here, :]
-        zonal = shift(we, halo(r, wide + levels, LANES - 1), False) - shift(
-            we, halo(r, levels, 0), True
+        zonal = shift(we, halo(hc, levels, r, wide + levels, LANES - 1), False) - shift(
+            we, halo(hc, levels, r, levels, 0), True
         )
         rhs = rhsb[:, :, here, :] - 0.5 * zonal
         rhs2b[:, :, here, :] = rhs
         cl = clb[:, :, here, :]
-        w_west = 0.5 * (cl + shift(cl, halo(r, 2 * levels, 0), True))
-        w_east = 0.5 * (cl + shift(cl, halo(r, wide + 2 * levels, LANES - 1), False))
+        w_west = 0.5 * (cl + shift(cl, halo(hc, levels, r, 2 * levels, 0), True))
+        w_east = 0.5 * (cl + shift(cl, halo(hc, levels, r, wide + 2 * levels, LANES - 1), False))
         wwb[:, :, here, :] = w_west
         ewb[:, :, here, :] = w_east
         total = totb[:, :, here, :] + w_west + w_east
         p = pb[:, :, mid, :]
         applied = appb[:, :, here, :]
-        applied += w_west * (p - shift(p, halo(r, 0, 0), True))
-        applied += w_east * (p - shift(p, halo(r, wide, LANES - 1), False))
+        applied += w_west * (p - shift(p, halo(hc, levels, r, 0, 0), True))
+        applied += w_east * (p - shift(p, halo(hc, levels, r, wide, LANES - 1), False))
         fresh = p + (rhs - applied) / total
         npb[:, :, mid, :] = fresh
         pk[here, :] = packed([fresh], narrow)
@@ -244,15 +294,6 @@
         accb[:, :, here, :] = rhs2b[:, :, here, :] - applied
         return 0
 
-    def second_outer(i, _):
-        r, here, mid, low, high = slices(i)
-        p = npb[:, :, mid, :]
-        acc = accb[:, :, here, :]
-        acc -= wwb[:, :, here, :] * (p - shift(p, halo(r, 0, 0), True))
-        acc -= ewb[:, :, here, :] * (p - shift(p, halo(r, narrow, LANES - 1), False))
-        resb[:, :, here, :] = acc
-        return 0
-
     def inner_rows(step, src, fields, phase):
         loop(1, chunks - 1, step)
         for slot in (2, 3):
@@ -271,27 +312,12 @@
     pack_rows((npb,), row2_send)
     sends += send_all(col2_send, col2_recv, row2_send, row2_recv, 1)
 
-    stores = []
-
-    def store(n, src, dst):
-        for t in range(tiles):
-            copy = pltpu.make_async_copy(
-                src(t), dst.at[:, :, pl.ds(t * LANES, LANES)], out_sem.at[n, t]
-            )
-            copy.start()
-            stores.append(copy)
-
-    store(0, lambda t: npb.at[:, t, pl.ds(SUB, rows), :], np_out)
     inner_rows(second_inner, row2_recv, (npb,), 1)
     for slot in (0, 1):
         wait_recv(col2_recv.at[slot], slot, 1)
     rows_to_columns(col2_recv, narrow)
-    loop(0, chunks, second_outer)
-    store(1, lambda t: resb.at[:, t], res_out)
     for copy in sends:
         copy.wait_send()
-    for copy in stores:
-        copy.wait()
 
 
 def lat_id(index, count):
@@ -309,28 +335,37 @@
     narrow = -(-levels // SUB) * SUB
     cols = lambda n: pltpu.VMEM((2, blocks, n, LANES), f32)
     edge = lambda n: pltpu.VMEM((2, tiles, n, LANES), f32)
-    shape = jax.ShapeDtypeStruct((levels, rows, width), f32)
     any_spec = pl.BlockSpec(memory_space=pl.ANY)
-    return pl.pallas_call(
+    vmem_spec = pl.BlockSpec(memory_space=pltpu.VMEM)
+    strip = pltpu.VMEM((blocks * LANES, LANES), f32)
+    held = pl.pallas_call(
         functools.partial(kernel, lon_n, lat_n, rows * lat_n),
-        out_shape=(shape, shape),
+        out_shape=(padded, plain, plain, plain, strip),
         in_specs=[any_spec] * 8,
-        out_specs=(any_spec, any_spec),
+        out_specs=(vmem_spec,) * 5,
         scratch_shapes=[
             padded, plain, padded, plain, plain, padded, plain, plain,
-            padded] + [plain] * 10 + [pltpu.VMEM((rows + SUB, LANES), f32),
-            pltpu.VMEM((blocks * LANES, LANES), f32), pltpu.VMEM((blocks * LANES, LANES), f32),
+        ] + [plain] * 6 + [
+            pltpu.VMEM((rows + SUB, LANES), f32), strip,
             cols(wide), cols(wide), edge(wide), edge(wide),
             cols(narrow), cols(narrow), edge(narrow), edge(narrow),
             pltpu.SemaphoreType.DMA((8, tiles)),
-            pltpu.SemaphoreType.DMA((2, tiles)),
             pltpu.SemaphoreType.DMA((2, 4)),
             pltpu.SemaphoreType.DMA((2, 4)),
         ],
         compiler_params=pltpu.CompilerParams(
-            collective_id=0, has_side_effects=True, vmem_limit_bytes=48 * 1024 * 1024
+            collective_id=0, has_side_effects=True, vmem_limit_bytes=44 * 1024 * 1024
         ),
     )(*(pltpu.with_memory_space_constraint(x, pltpu.HBM) for x in fields))
+    result = pltpu.HBM((levels, rows, width), f32)
+    return pl.pallas_call(
+        functools.partial(finish, narrow),
+        out_shape=(result, result),
+        in_specs=[vmem_spec] * 5,
+        out_specs=(any_spec, any_spec),
+        scratch_shapes=[plain, pltpu.SemaphoreType.DMA((2, 3, tiles))],
+        compiler_params=pltpu.CompilerParams(vmem_limit_bytes=16 * 1024 * 1024),
+    )(*(pltpu.with_memory_space_constraint(x, pltpu.VMEM) for x in held))
 
 
 def solution(mesh):

time: 23.6 us -> 22.4 us (0.949)
  local copies, waits for them, and re-layouts: 1.89 us -> 0 us
  Pallas kernels: 20.9 us -> 21.6 us
    pallas_call x0 -> x1, Pallas kernels: none -> 2.01 us  [per_device(): pl.pallas_call(functools.partial(finish, narrow), out_shape=(result, resu...]
    unnamed x2 -> x0, local copies, waits for them, and re-layouts: 1.89 us -> none
    pallas_call x1, Pallas kernels: 20.9 us -> 19.6 us  [per_device(): pl.pallas_call(functools.partial(kernel, lon_n, lat_n, rows * lat_n), out...]
where the time goes in v3:
time: 22.4 us; the launch traced here: 22.3 us
  Pallas kernels  21.6 us (96%)
  between operations  0.64 us (3%)
    pallas_call x1, Pallas kernels, per_device(): pl.pallas_call(functools.partial(kernel, lon_n, lat_n, rows * lat_n), out...  19.6 us
    pallas_call x1, Pallas kernels, per_device(): pl.pallas_call(functools.partial(finish, narrow), out_shape=(result, resu...  2.01 us

profile of v3, /device:TPU:0, one launch (start us, length us, event | category | flops | bytes accessed | tf_op | source)
XLA Modules:
  0.0 22.3 jit_solution(17223149897965179648)
XLA Ops:
  0.6 19.6 %shard_map.95 = (f32[4,2,256,128]{3,2,1,0:T(8,128)S(1)}, f32[4,2,240,128]{3,2,1,0:T(8,128)S(1)}, f32[4,2,240,128]{3,2,1,0:T(8,128)S(1)}, f32[4,2,240,128]{3,2,1,0:T(8,128)S(1)}, f32[256,128]{1,0:T(8,128)S(1)}) custom-call(f32[4,240,256]{2,1,0:T(8,128)} %p_in.1, f32[4,240,256]{2,1,0:T(8,128)} %we_in.1, f32[4,240,256]{2,1,0:T(8,128)} %wn_in.1, ...), custom_call_target="tpu_custom_call" | custom-call | tf_op jit(solution)/shard_map/pallas_call | solution.py:341
  20.3 2.0 %shard_map.96 = (f32[4,240,256]{2,1,0:T(8,128)}, f32[4,240,256]{2,1,0:T(8,128)}) custom-call(f32[4,2,256,128]{3,2,1,0:T(8,128)S(1)} %get-tuple-element.7.npb, f32[4,2,240,128]{3,2,1,0:T(8,128)S(1)} %get-tuple-element.8.accb, f32[4,2,240,128]{3,2,1,0:T(8,128)S(1)} %get-tuple-element.9.wwb, f32[4,2,240,128]{3,2,1,0:T(8,128)S(1)} %get-tuple-element.10.ewb, ...), custom_call_target="tpu_custom_call" | custom-call | tf_op jit(solution)/shard_map/pallas_call | solution.py:361

commit v4 on v3

--- a/solution.py
+++ b/solution.py
@@ -23,11 +23,8 @@
     return r, pl.ds(r, SUB), pl.ds(r + SUB, SUB), pl.ds(r + SUB - 1, SUB), pl.ds(r + SUB + 1, SUB)
 
 
-def halo(hc, levels, r, first, target):
-    edge = hc[pl.ds(r, SUB), :]
-    return jnp.stack(
-        [pltpu.roll(edge, (target - first - k) % LANES, 1) for k in range(levels)]
-    )[:, None]
+def strip_column(hc, r, lane_from, target):
+    return pltpu.roll(hc[pl.ds(r, SUB), :], (target - lane_from) % LANES, 1)
 
 
 def shift(x, rim, west_side):
@@ -48,7 +45,7 @@
     return flux - jnp.concatenate((flux[1:], jnp.zeros_like(p[:1])), 0)
 
 
-def finish(narrow, npb, accb, wwb, ewb, hc, np_out, res_out, resb, sem):
+def finish(narrow, npb, accb, hc, np_out, res_out, resb, sem):
     levels, tiles, rows = accb.shape[0], accb.shape[1], accb.shape[2]
     chunks = rows // SUB
     parts = max(n for n in range(1, 4) if chunks % n == 0)
@@ -65,15 +62,18 @@
             copy.start()
             copies.append(copy)
 
+    lane = lax.broadcasted_iota(jnp.int32, (SUB, LANES), 1)
+
     def step(i, _):
         r, here, mid, low, high = slices(i)
-        p = npb[:, :, mid, :]
-        acc = accb[:, :, here, :]
-        acc -= wwb[:, :, here, :] * (p - shift(p, halo(hc, levels, r, 0, 0), True))
-        acc -= ewb[:, :, here, :] * (
-            p - shift(p, halo(hc, levels, r, narrow, LANES - 1), False)
-        )
-        resb[:, :, here, :] = acc
+        for k in range(levels):
+            for t in range(tiles):
+                acc = accb[k, t, here, :]
+                if t == 0:
+                    acc += jnp.where(lane == 0, strip_column(hc, r, narrow + k, 0), 0.0)
+                if t == tiles - 1:
+                    acc += jnp.where(lane == LANES - 1, strip_column(hc, r, k, LANES - 1), 0.0)
+                resb[k, t, here, :] = acc
         return 0
 
     for part in range(parts):
@@ -88,10 +88,10 @@
 def kernel(
     lon_n, lat_n, lat_total,
     p_in, we_in, wn_in, f_in, cl_in, ct_in, cv_in, dg_in,
-    npb, accb, wwb, ewb, hc,
+    npb, accb, hc,
     pb, web, wnb, fb, clb, ctb, cvb, dgb,
-    rhsb, rhs2b, appb, totb, swb, nwb, cosb,
-    pk, col_send, col_recv, row_send, row_recv,
+    rhsb, wwb, ewb, swb, nwb, cosb,
+    pk, part, fix, col_send, col_recv, row_send, row_recv,
     col2_send, col2_recv, row2_send, row2_recv,
     in_sem, send_sem, recv_sem,
 ):
@@ -194,10 +194,14 @@
     south_slot = 1 - at_south
     north_slot = at_north
 
-    def send_all(cs, cr, rs, rr, phase):
+    def send_columns(cs, cr, phase):
         return (
             send(0, cs.at[0], cr.at[0], east, 0, phase),
             send(1, cs.at[1], cr.at[1], west, 1, phase),
+        )
+
+    def send_rows(rs, rr, phase):
+        return (
             send(2, rs.at[0], rr.at[south_slot], south, 2 + south_slot, phase),
             send(3, rs.at[1], rr.at[north_slot], north, 2 + north_slot, phase),
         )
@@ -224,29 +228,42 @@
         )
     wide = col_send.shape[2]
     narrow = col2_send.shape[2]
+    pair = part.shape[2]
     row_send[...] = jnp.zeros(row_send.shape, jnp.float32)
     row2_send[...] = jnp.zeros(row2_send.shape, jnp.float32)
+    col2_send[...] = jnp.zeros(col2_send.shape, jnp.float32)
+    fix[...] = jnp.zeros(fix.shape, jnp.float32)
 
     wait_load(0, 1, 2)
     start_load(5, 6, 7)
     loop(0, chunks, pack_first)
     columns_to_rows(col_send, wide)
+    pl.semaphore_wait(barrier, len(partners))
+    sends = send_columns(col_send, col_recv, 0)
     wait_load(3, 4)
     pack_rows((pb, wnb, ctb), row_send)
-    pl.semaphore_wait(barrier, len(partners))
-    sends = send_all(col_send, col_recv, row_send, row_recv, 0)
+    sends += send_rows(row_send, row_recv, 0)
 
     wait_load(5, 6, 7)
 
-    def first_inner(i, _):
+    def first_pass(i, _):
         r, here, mid, low, high = slices(i)
         c_low = cosb[here, :]
         c_high = cosb[pl.ds(r + 1, SUB), :]
         m_low = 0.25 * (1.0 + jnp.abs(c_low))
         m_high = 0.25 * (1.0 + jnp.abs(c_high))
+        we = web[:, :, here, :]
+        none = jnp.zeros_like(we[:, :1])
+        zonal = shift(we, none, False) - shift(we, none, True)
         wn = wnb[:, :, mid, :]
         merid = c_high * (wn + wnb[:, :, high, :]) - c_low * (wnb[:, :, low, :] + wn)
-        rhsb[:, :, here, :] = fb[:, :, here, :] - 0.5 * merid
+        rhs = fb[:, :, here, :] - 0.5 * (zonal + merid)
+        rhsb[:, :, here, :] = rhs
+        cl = clb[:, :, here, :]
+        w_west = 0.5 * (cl + shift(cl, -cl[:, :1], True))
+        w_east = 0.5 * (cl + shift(cl, -cl[:, -1:], False))
+        wwb[:, :, here, :] = w_west
+        ewb[:, :, here, :] = w_east
         ct = ctb[:, :, mid, :]
         w_south = m_low * (ct + ctb[:, :, low, :])
         w_north = m_high * (ct + ctb[:, :, high, :])
@@ -255,43 +272,39 @@
         v = cvb[:, :, here, :]
         dg = dgb[:, :, here, :]
         upper = jnp.concatenate((v[1:], jnp.zeros_like(v[:1])), 0)
-        totb[:, :, here, :] = dg + w_south + w_north + v + upper
+        total = dg + w_west + w_east + w_south + w_north + v + upper
         p = pb[:, :, mid, :]
         applied = dg * p + vertical(p, v)
+        applied += w_west * (p - shift(p, none, True))
+        applied += w_east * (p - shift(p, none, False))
         applied += w_south * (p - pb[:, :, low, :])
-        appb[:, :, here, :] = applied + w_north * (p - pb[:, :, high, :])
+        applied += w_north * (p - pb[:, :, high, :])
+        short = rhs - applied
+        npb[:, :, mid, :] = p + short / total
+        pk[here, :] = packed([short, total], pair)
         return 0
 
-    def first_outer(i, _):
+    def merge(i, _):
         r, here, mid, low, high = slices(i)
-        we = web[:, :, here, :]
-        zonal = shift(we, halo(hc, levels, r, wide + levels, LANES - 1), False) - shift(
-            we, halo(hc, levels, r, levels, 0), True
-        )
-        rhs = rhsb[:, :, here, :] - 0.5 * zonal
-        rhs2b[:, :, here, :] = rhs
-        cl = clb[:, :, here, :]
-        w_west = 0.5 * (cl + shift(cl, halo(hc, levels, r, 2 * levels, 0), True))
-        w_east = 0.5 * (cl + shift(cl, halo(hc, levels, r, wide + 2 * levels, LANES - 1), False))
-        wwb[:, :, here, :] = w_west
-        ewb[:, :, here, :] = w_east
-        total = totb[:, :, here, :] + w_west + w_east
-        p = pb[:, :, mid, :]
-        applied = appb[:, :, here, :]
-        applied += w_west * (p - shift(p, halo(hc, levels, r, 0, 0), True))
-        applied += w_east * (p - shift(p, halo(hc, levels, r, wide, LANES - 1), False))
-        fresh = p + (rhs - applied) / total
-        npb[:, :, mid, :] = fresh
-        pk[here, :] = packed([fresh], narrow)
+        for k in range(levels):
+            npb[k, 0, mid, :] = jnp.where(
+                lane == 0, strip_column(hc, r, narrow + k, 0), npb[k, 0, mid, :]
+            )
+            npb[k, tiles - 1, mid, :] = jnp.where(
+                lane == LANES - 1, strip_column(hc, r, k, LANES - 1), npb[k, tiles - 1, mid, :]
+            )
         return 0
 
-    def second_inner(i, _):
+    def second_pass(i, _):
         r, here, mid, low, high = slices(i)
         p = npb[:, :, mid, :]
+        none = jnp.zeros_like(p[:, :1])
         applied = dgb[:, :, here, :] * p + vertical(p, cvb[:, :, here, :])
+        applied += wwb[:, :, here, :] * (p - shift(p, none, True))
+        applied += ewb[:, :, here, :] * (p - shift(p, none, False))
         applied += swb[:, :, here, :] * (p - npb[:, :, low, :])
         applied += nwb[:, :, here, :] * (p - npb[:, :, high, :])
-        accb[:, :, here, :] = rhs2b[:, :, here, :] - applied
+        accb[:, :, here, :] = rhsb[:, :, here, :] - applied
         return 0
 
     def inner_rows(step, src, fields, phase):
@@ -302,20 +315,35 @@
         step(0, 0)
         step(chunks - 1, 0)
 
-    inner_rows(first_inner, row_recv, (pb, wnb, ctb), 0)
+    inner_rows(first_pass, row_recv, (pb, wnb, ctb), 0)
+    columns_to_rows(part, pair)
     for slot in (0, 1):
         wait_recv(col_recv.at[slot], slot, 0)
-    rows_to_columns(col_recv, wide)
-    loop(0, chunks, first_outer)
-
-    columns_to_rows(col2_send, narrow)
+
+    edges = []
+    for side in (0, 1):
+        for u in range(blocks):
+            own, other = col_send[side, u], col_recv[1 - side, u]
+            p = own[:levels]
+            weight = 0.5 * (own[2 * levels:3 * levels] + other[2 * levels:3 * levels])
+            gain = (side - 0.5) * other[levels:2 * levels]
+            short = part[side, u, :levels, :] + gain - weight * (p - other[:levels])
+            total = part[side, u, levels:2 * levels, :] + weight
+            fresh = p + short / jnp.where(total > 0.0, total, 1.0)
+            col2_send[side, u, :levels, :] = fresh
+            edges.append((side, u, weight, gain, fresh))
+    sends += send_columns(col2_send, col2_recv, 1)
+    rows_to_columns(col2_send, narrow)
+    loop(0, chunks, merge)
     pack_rows((npb,), row2_send)
-    sends += send_all(col2_send, col2_recv, row2_send, row2_recv, 1)
-
-    inner_rows(second_inner, row2_recv, (npb,), 1)
+    sends += send_rows(row2_send, row2_recv, 1)
+
+    inner_rows(second_pass, row2_recv, (npb,), 1)
     for slot in (0, 1):
         wait_recv(col2_recv.at[slot], slot, 1)
-    rows_to_columns(col2_recv, narrow)
+    for side, u, weight, gain, fresh in edges:
+        fix[side, u, :levels, :] = gain - weight * (fresh - col2_recv[1 - side, u, :levels, :])
+    rows_to_columns(fix, narrow)
     for copy in sends:
         copy.wait_send()
 
@@ -333,6 +361,7 @@
     padded = pltpu.VMEM((levels, tiles, rows + 2 * SUB, LANES), f32)
     wide = -(-3 * levels // SUB) * SUB
     narrow = -(-levels // SUB) * SUB
+    pair = -(-2 * levels // SUB) * SUB
     cols = lambda n: pltpu.VMEM((2, blocks, n, LANES), f32)
     edge = lambda n: pltpu.VMEM((2, tiles, n, LANES), f32)
     any_spec = pl.BlockSpec(memory_space=pl.ANY)
@@ -340,13 +369,13 @@
     strip = pltpu.VMEM((blocks * LANES, LANES), f32)
     held = pl.pallas_call(
         functools.partial(kernel, lon_n, lat_n, rows * lat_n),
-        out_shape=(padded, plain, plain, plain, strip),
+        out_shape=(padded, plain, strip),
         in_specs=[any_spec] * 8,
-        out_specs=(vmem_spec,) * 5,
+        out_specs=(vmem_spec,) * 3,
         scratch_shapes=[
             padded, plain, padded, plain, plain, padded, plain, plain,
-        ] + [plain] * 6 + [
-            pltpu.VMEM((rows + SUB, LANES), f32), strip,
+        ] + [plain] * 5 + [
+            pltpu.VMEM((rows + SUB, LANES), f32), strip, cols(pair), cols(narrow),
             cols(wide), cols(wide), edge(wide), edge(wide),
             cols(narrow), cols(narrow), edge(narrow), edge(narrow),
             pltpu.SemaphoreType.DMA((8, tiles)),
@@ -361,7 +390,7 @@
     return pl.pallas_call(
         functools.partial(finish, narrow),
         out_shape=(result, result),
-        in_specs=[vmem_spec] * 5,
+        in_specs=[vmem_spec] * 3,
         out_specs=(any_spec, any_spec),
         scratch_shapes=[plain, pltpu.SemaphoreType.DMA((2, 3, tiles))],
         compiler_params=pltpu.CompilerParams(vmem_limit_bytes=16 * 1024 * 1024),

time: 22.4 us -> 18.4 us (0.82)
  Pallas kernels: 21.6 us -> 17.6 us
    pallas_call x1, Pallas kernels: 19.6 us -> 16.1 us  [per_device(): pl.pallas_call(functools.partial(kernel, lon_n, lat_n, rows * lat_n), out...]
    pallas_call x1, Pallas kernels: 2.01 us -> 1.52 us  [per_device(): pl.pallas_call(functools.partial(finish, narrow), out_shape=(result, resu...]
where the time goes in v4:
time: 18.4 us; the launch traced here: 18.3 us
  Pallas kernels  17.6 us (96%)
  between operations  0.64 us (3%)
    pallas_call x1, Pallas kernels, per_device(): pl.pallas_call(functools.partial(kernel, lon_n, lat_n, rows * lat_n), out...  16.1 us
    pallas_call x1, Pallas kernels, per_device(): pl.pallas_call(functools.partial(finish, narrow), out_shape=(result, resu...  1.52 us

profile of v4, /device:TPU:0, one launch (start us, length us, event | category | flops | bytes accessed | tf_op | source)
XLA Modules:
  0.0 18.3 jit_solution(145477991027286235)
XLA Ops:
  0.6 16.1 %shard_map.95 = (f32[4,2,256,128]{3,2,1,0:T(8,128)S(1)}, f32[4,2,240,128]{3,2,1,0:T(8,128)S(1)}, f32[256,128]{1,0:T(8,128)S(1)}) custom-call(f32[4,240,256]{2,1,0:T(8,128)} %p_in.1, f32[4,240,256]{2,1,0:T(8,128)} %we_in.1, f32[4,240,256]{2,1,0:T(8,128)} %wn_in.1, f32[4,240,256]{2,1,0:T(8,128)} %f_in.1, f32[4,240,256]{2,1,0:T(8,128)} %cl_in.1, ...), custom_call_target="tpu_custom_call" | custom-call | tf_op jit(solution)/shard_map/pallas_call | solution.py:370
  16.7 1.5 %shard_map.96 = (f32[4,240,256]{2,1,0:T(8,128)}, f32[4,240,256]{2,1,0:T(8,128)}) custom-call(f32[4,2,256,128]{3,2,1,0:T(8,128)S(1)} %get-tuple-element.5.npb, f32[4,2,240,128]{3,2,1,0:T(8,128)S(1)} %get-tuple-element.6.accb, f32[256,128]{1,0:T(8,128)S(1)} %get-tuple-element.7.hc), custom_call_target="tpu_custom_call" | custom-call | tf_op jit(solution)/shard_map/pallas_call | solution.py:390

commit v5 on v4

--- a/solution.py
+++ b/solution.py
@@ -129,7 +129,7 @@
             for copy in loads[a]:
                 copy.start()
 
-    start_load(0, 1, 2, 3, 4)
+    start_load(0, 1, 2)
 
     barrier = pltpu.get_barrier_semaphore()
     for lo, la in partners:
@@ -234,7 +234,9 @@
     col2_send[...] = jnp.zeros(col2_send.shape, jnp.float32)
     fix[...] = jnp.zeros(fix.shape, jnp.float32)
 
-    wait_load(0, 1, 2)
+    wait_load(0)
+    start_load(3, 4)
+    wait_load(1, 2)
     start_load(5, 6, 7)
     loop(0, chunks, pack_first)
     columns_to_rows(col_send, wide)
@@ -334,9 +336,11 @@
             edges.append((side, u, weight, gain, fresh))
     sends += send_columns(col2_send, col2_recv, 1)
     rows_to_columns(col2_send, narrow)
-    loop(0, chunks, merge)
+    merge(0, 0)
+    merge(chunks - 1, 0)
     pack_rows((npb,), row2_send)
     sends += send_rows(row2_send, row2_recv, 1)
+    loop(1, chunks - 1, merge)
 
     inner_rows(second_pass, row2_recv, (npb,), 1)
     for slot in (0, 1):

time: 18.4 us -> 18.4 us (level)
  no operation moved by 1% of the time
where the time goes in v5:
time: 18.4 us; the launch traced here: 18.2 us
  Pallas kernels  17.6 us (96%)
  between operations  0.64 us (3%)
    pallas_call x1, Pallas kernels, per_device(): pl.pallas_call(functools.partial(kernel, lon_n, lat_n, rows * lat_n), out...  16.1 us
    pallas_call x1, Pallas kernels, per_device(): pl.pallas_call(functools.partial(finish, narrow), out_shape=(result, resu...  1.52 us

profile of v5, /device:TPU:0, one launch (start us, length us, event | category | flops | bytes accessed | tf_op | source)
XLA Modules:
  0.0 18.2 jit_solution(13537105790231208187)
XLA Ops:
  0.6 16.1 %shard_map.95 = (f32[4,2,256,128]{3,2,1,0:T(8,128)S(1)}, f32[4,2,240,128]{3,2,1,0:T(8,128)S(1)}, f32[256,128]{1,0:T(8,128)S(1)}) custom-call(f32[4,240,256]{2,1,0:T(8,128)} %p_in.1, f32[4,240,256]{2,1,0:T(8,128)} %we_in.1, f32[4,240,256]{2,1,0:T(8,128)} %wn_in.1, f32[4,240,256]{2,1,0:T(8,128)} %f_in.1, f32[4,240,256]{2,1,0:T(8,128)} %cl_in.1, ...), custom_call_target="tpu_custom_call" | custom-call | tf_op jit(solution)/shard_map/pallas_call | solution.py:374
  16.7 1.5 %shard_map.96 = (f32[4,240,256]{2,1,0:T(8,128)}, f32[4,240,256]{2,1,0:T(8,128)}) custom-call(f32[4,2,256,128]{3,2,1,0:T(8,128)S(1)} %get-tuple-element.5.npb, f32[4,2,240,128]{3,2,1,0:T(8,128)S(1)} %get-tuple-element.6.accb, f32[256,128]{1,0:T(8,128)S(1)} %get-tuple-element.7.hc), custom_call_target="tpu_custom_call" | custom-call | tf_op jit(solution)/shard_map/pallas_call | solution.py:394

commit v6 on v5

--- a/solution.py
+++ b/solution.py
@@ -14,7 +14,7 @@
 
 
 def loop(first, last, step):
-    size = max(n for n in range(1, 6) if (last - first) % n == 0)
+    size = max(n for n in range(1, 3) if (last - first) % n == 0)
     lax.fori_loop(first, last, step, 0, unroll=size)
 
 

time: 18.4 us -> 19.1 us (1.038)
  Pallas kernels: 17.6 us -> 18.3 us
    pallas_call x1, Pallas kernels: 1.52 us -> 2.13 us  [per_device(): pl.pallas_call(functools.partial(finish, narrow), out_shape=(result, resu...]
where the time goes in v6:
time: 19.1 us; the launch traced here: 18.9 us
  Pallas kernels  18.3 us (96%)
  between operations  0.64 us (3%)
    pallas_call x1, Pallas kernels, per_device(): pl.pallas_call(functools.partial(kernel, lon_n, lat_n, rows * lat_n), out...  16.2 us
    pallas_call x1, Pallas kernels, per_device(): pl.pallas_call(functools.partial(finish, narrow), out_shape=(result, resu...  2.13 us

profile of v6, /device:TPU:0, one launch (start us, length us, event | category | flops | bytes accessed | tf_op | source)
XLA Modules:
  0.0 18.9 jit_solution(5146821603620196185)
XLA Ops:
  0.6 16.2 %shard_map.95 = (f32[4,2,256,128]{3,2,1,0:T(8,128)S(1)}, f32[4,2,240,128]{3,2,1,0:T(8,128)S(1)}, f32[256,128]{1,0:T(8,128)S(1)}) custom-call(f32[4,240,256]{2,1,0:T(8,128)} %p_in.1, f32[4,240,256]{2,1,0:T(8,128)} %we_in.1, f32[4,240,256]{2,1,0:T(8,128)} %wn_in.1, f32[4,240,256]{2,1,0:T(8,128)} %f_in.1, f32[4,240,256]{2,1,0:T(8,128)} %cl_in.1, ...), custom_call_target="tpu_custom_call" | custom-call | tf_op jit(solution)/shard_map/pallas_call | solution.py:374
  16.8 2.1 %shard_map.96 = (f32[4,240,256]{2,1,0:T(8,128)}, f32[4,240,256]{2,1,0:T(8,128)}) custom-call(f32[4,2,256,128]{3,2,1,0:T(8,128)S(1)} %get-tuple-element.5.npb, f32[4,2,240,128]{3,2,1,0:T(8,128)S(1)} %get-tuple-element.6.accb, f32[256,128]{1,0:T(8,128)S(1)} %get-tuple-element.7.hc), custom_call_target="tpu_custom_call" | custom-call | tf_op jit(solution)/shard_map/pallas_call | solution.py:394
